TPU v7x, 32 devices: a whole 2x2x4 slice. The times are simulated.
32 devices in a mesh: ctx: 8 (over z, x), uly: 4 (over y, core).
Axes of the slice: x: 2, y: 2, z: 4, core: 2. Of those that a mesh axis runs over, the one named last changes fastest.
Arguments:
- q_new: bfloat16 [512, 4096], P(('ctx', 'uly')), may hold values from -20 to 20
- k_new: bfloat16 [512, 4096], P(('ctx', 'uly')), may hold values from -6 to 6
- v_new: bfloat16 [512, 4096], P(('ctx', 'uly')), may hold values from -6 to 6
- cache_k: bfloat16 [8192, 4096], P('ctx', 'uly'), may hold values from -4 to 4
- cache_v: bfloat16 [8192, 4096], P('ctx', 'uly'), may hold values from -6 to 6
- filled_slots: int32 [1], replicated, may hold values from 4097 to 8192
- norm_gain: float32 [4096], replicated, may hold values from 0.1 to 1.9
- v_branch: bfloat16 [512, 4096], P(('ctx', 'uly')), may hold values from -6 to 6
- x_gate: bfloat16 [512, 4096], P(('ctx', 'uly')), may hold values from -6 to 6
- conv_state: bfloat16 [6, 4096], replicated, may hold values from -6 to 6
- conv_filter: float32 [7, 256], replicated, may hold values from -2 to 2
- skip_gain: float32 [4096], replicated, may hold values from -1 to 1
Outputs:
- mixed: bfloat16 [512, 4096], P(('ctx', 'uly'))
All inputs are finite; a program needn't handle non-finite values.
Results may differ from a plain program's by a relative error of at most 0.04.
Values may be sent and summed in bfloat16 or wider, within the bound.
No kernel may reach another device: no remote copies, remote signals or barrier semaphores. Data moves between devices by JAX's collectives and lax.ppermute only.
A program may use at most 128 MiB of HBM per device.

v0:
```python
import math

import jax
import jax.numpy as jnp
from jax import lax
from jax.sharding import PartitionSpec as P

DH = 128


def shifted(block, axis, distance):
    devices = range(lax.axis_size(axis))
    route = [(i - distance, i) for i in devices if i - distance in devices]
    return lax.ppermute(block, axis, route)


def online(carried, queries, key_rows, value_rows, valid_mask):
    running_max, running_sum, running_out = carried
    head_count = running_max.shape[1]
    query_heads = queries.reshape(queries.shape[0], head_count, -1)
    key_heads = key_rows.reshape(key_rows.shape[0], head_count, -1)
    value_heads = value_rows.reshape(value_rows.shape[0], head_count, -1)
    score_scale = 1.0 / math.sqrt(query_heads.shape[2])
    scores = (
        jnp.einsum("qhd,khd->qhk", query_heads, key_heads, preferred_element_type=jnp.float32)
        * score_scale
    )
    scores = jnp.where(valid_mask[:, None, :], scores, -jnp.inf)
    new_max = jnp.maximum(running_max, jnp.max(scores, axis=2))
    usable = jnp.where(jnp.isfinite(new_max), new_max, 0.0)
    factor = jnp.exp(running_max - usable)
    weights = jnp.exp(scores - usable[:, :, None])
    running_sum = running_sum * factor + jnp.sum(weights, axis=2)
    running_out = running_out * factor[:, :, None] + jnp.einsum(
        "qhk,khd->qhd",
        weights.astype(jnp.bfloat16),
        value_heads,
        preferred_element_type=jnp.float32,
    )
    return (new_max, running_sum, running_out)


def blocked(carried, key_rows, value_rows, first_row, update):
    key_count = key_rows.shape[0]
    block_width = math.gcd(key_count, 1024)
    block_count = key_count // block_width
    if block_count == 1:
        return update(carried, key_rows, value_rows, first_row)

    def advance(block_index, softmax_state):
        offset = block_index * block_width
        return update(
            softmax_state,
            lax.dynamic_slice_in_dim(key_rows, offset, block_width, 0),
            lax.dynamic_slice_in_dim(value_rows, offset, block_width, 0),
            offset,
        )

    return lax.fori_loop(0, block_count, advance, carried)


def cache_update(queries, cache_limit):

    def update(carried, key_rows, value_rows, first_row):
        slot_ids = first_row + lax.iota(jnp.int32, key_rows.shape[0])
        valid_mask = jnp.broadcast_to(
            (slot_ids < cache_limit)[None, :], (queries.shape[0], key_rows.shape[0])
        )
        return online(carried, queries, key_rows, value_rows, valid_mask)

    return update


def fresh_update(queries, positions):

    def update(carried, key_rows, value_rows, first_row):
        slot_ids = first_row + lax.iota(jnp.int32, key_rows.shape[0])
        return online(
            carried, queries, key_rows, value_rows, slot_ids[None, :] <= positions[:, None]
        )

    return update


def empty_state(query_rows, head_count, head_width):
    return (
        jnp.full((query_rows, head_count), -jnp.inf, jnp.float32),
        jnp.zeros((query_rows, head_count), jnp.float32),
        jnp.zeros((query_rows, head_count, head_width), jnp.float32),
    )


def body(
    q_new,
    k_new,
    v_new,
    cache_k,
    cache_v,
    filled_slots,
    norm_gain,
    v_branch,
    x_gate,
    conv_state,
    conv_filter,
    skip_gain,
):
    queries, keys_here, values_here = (
        lax.all_to_all(q_new, "uly", split_axis=1, concat_axis=0, tiled=True),
        lax.all_to_all(k_new, "uly", split_axis=1, concat_axis=0, tiled=True),
        lax.all_to_all(v_new, "uly", split_axis=1, concat_axis=0, tiled=True),
    )
    query_rows, width_all = queries.shape
    head_count = width_all // DH
    cache_limit = filled_slots[0]
    ctx_index = lax.axis_index("ctx")
    positions = ctx_index * query_rows + lax.iota(jnp.int32, query_rows)
    softmax_state = empty_state(query_rows, head_count, DH)
    pieces = (
        lax.all_gather(cache_k, "ctx", axis=0, tiled=True),
        lax.all_gather(cache_v, "ctx", axis=0, tiled=True),
    )
    softmax_state = blocked(
        softmax_state, pieces[0], pieces[1], jnp.int32(0), cache_update(queries, cache_limit)
    )
    pieces = (
        lax.all_gather(keys_here, "ctx", axis=0, tiled=True),
        lax.all_gather(values_here, "ctx", axis=0, tiled=True),
    )
    running_max, running_sum, running_out = blocked(
        softmax_state, pieces[0], pieces[1], jnp.int32(0), fresh_update(queries, positions)
    )
    attended = (
        (running_out / running_sum[:, :, None]).reshape(query_rows, width_all).astype(jnp.bfloat16)
    )
    token_rows = lax.all_to_all(attended, "uly", split_axis=0, concat_axis=1, tiled=True)
    values32 = token_rows.astype(jnp.float32)
    normed = (
        values32
        * lax.rsqrt(jnp.mean(values32 * values32, axis=1, keepdims=True) + 1e-06)
        * norm_gain
    )
    conv_input = lax.optimization_barrier(
        (normed * v_branch.astype(jnp.float32)).astype(jnp.bfloat16)
    )
    conv_reach = conv_filter.shape[0] - 1
    incoming = shifted(conv_input[-conv_reach:], ("ctx", "uly"), 1)
    first_device = jnp.logical_and(lax.axis_index("ctx") == 0, lax.axis_index("uly") == 0)
    lower_rim = jnp.where(first_device, conv_state, incoming)
    extended = jnp.concatenate([lower_rim, conv_input], axis=0).astype(jnp.float32)
    tap_table = jnp.repeat(conv_filter, conv_input.shape[1] // conv_filter.shape[1], axis=1)
    token_count = conv_input.shape[0]
    filtered = tap_table[0] * extended[conv_reach : conv_reach + token_count]
    for shift_lag in range(1, conv_reach + 1):
        filtered = (
            filtered
            + tap_table[shift_lag]
            * extended[conv_reach - shift_lag : conv_reach - shift_lag + token_count]
        )
    result = x_gate.astype(jnp.float32) * (filtered + skip_gain * conv_input.astype(jnp.float32))
    return result.astype(jnp.bfloat16)


def solution(mesh):
    in_specs = (
        P(("ctx", "uly"), None),
        P(("ctx", "uly"), None),
        P(("ctx", "uly"), None),
        P("ctx", "uly"),
        P("ctx", "uly"),
        P(),
        P(),
        P(("ctx", "uly"), None),
        P(("ctx", "uly"), None),
        P(),
        P(),
        P(),
    )
    out_specs = P(("ctx", "uly"), None)
    return jax.shard_map(body, mesh=mesh, in_specs=in_specs, out_specs=out_specs, check_vma=False)
```

profile of v0, /device:TPU:8, one launch (start us, length us, event | category | flops | bytes accessed | tf_op | source)
XLA Modules:
  0.0 651.5 jit_solution(15406224602365150429)
XLA Ops:
  6.5 0.9 copy.81
  7.5 7.7 %all_to_all.67 = bf16[16,4,1024]{2,0,1:T(8,128)(2,1)} all-to-all(bf16[16,4,1024]{2,0,1:T(8,128)(2,1)S(1)} %bitcast.109), channel_id=1, replica_groups=mesh['ctx'=8,'uly'=4] {'uly'}, dimensions={1} | all-to-all | bytes 262144 | tf_op jit(solution)/shard_map/all_to_all | solution.py:109
  15.2 0.9 copy.80
  16.1 7.7 %all_to_all.68 = bf16[16,4,1024]{2,0,1:T(8,128)(2,1)} all-to-all(bf16[16,4,1024]{2,0,1:T(8,128)(2,1)S(1)} %bitcast.110), channel_id=1, replica_groups=mesh['ctx'=8,'uly'=4] {'uly'}, dimensions={1} | all-to-all | bytes 262144 | tf_op jit(solution)/shard_map/all_to_all | solution.py:110
  23.9 4.0 copy.45
  27.9 1.5 copy-done.1
  29.4 2.6 copy.47
  32.0 0.9 copy-done.4
  32.9 0.7 copy.82
  33.6 3.3 all-to-all-start
  37.0 4.5 all-to-all-done
  41.5 13.2 %all-gather.9.cloned.1.call-done = bf16[512,1024]{1,0:T(8,128)(2,1)} async-done(((bf16[64,1024]{1,0:T(8,128)(2,1)}), bf16[512,1024]{1,0:T(8,128)(2,1)}) %all-gather.9.cloned.1.call-update) | async-done | bytes 1048592 | tf_op jit(solution)/shard_map/all_gather | solution.py:126
  54.8 1.5 copy.49
  56.3 39.6 %all-gather.11.cloned.1.call-done = bf16[512,1024]{1,0:T(8,128)(2,1)} async-done(((bf16[64,1024]{1,0:T(8,128)(2,1)}), bf16[512,1024]{1,0:T(8,128)(2,1)}) %all-gather.11.cloned.1.call-update) | async-done | bytes 1048592 | tf_op jit(solution)/shard_map/all_gather | solution.py:127
  95.8 2.3 copy.53
  98.5 225.0 %all-gather.5.cloned.1.call-done = bf16[8192,1024]{0,1:T(8,128)(2,1)} async-done(((bf16[1024,1024]{0,1:T(8,128)(2,1)}), bf16[8192,1024]{0,1:T(8,128)(2,1)}) %all-gather.5.cloned.1.call-update) | async-done | bytes 16777232 | tf_op jit(solution)/shard_map/all_gather | solution.py:119
  323.5 227.8 %all-gather.7.cloned.1.call-done = bf16[8192,1024]{0,1:T(8,128)(2,1)} async-done(((bf16[1024,1024]{0,1:T(8,128)(2,1)}), bf16[8192,1024]{0,1:T(8,128)(2,1)}) %all-gather.7.cloned.1.call-update) | async-done | bytes 16777232 | tf_op jit(solution)/shard_map/all_gather | solution.py:120
  551.4 75.1 %while.18 = (s32[]{:T(128)}, f32[64,8]{0,1:T(8,128)S(1)}, f32[64,8]{0,1:T(8,128)S(1)}, f32[64,8,128]{2,0,1:T(8,128)}, s32[]{:T(128)}, /*index=5*/bf16[8192,1024]...) while((s32[]{:T(128)}, f32[64,8]{0,1:T(8,128)S(1)}, ...), condition=%wide.region_3.4_spmd.clone, body=%wide.region_0.3_spmd.clone.sunk | while | flops 274405888 | bytes 27957460 | solution.py:59
  551.4 4.0 constant_dynamic-slice_fusion.3
  555.3 0.7 add_compare_fusion.2
  557.2 1.0 copy-done
  558.2 1.7 fusion.55
  559.9 4.0 constant_dynamic-slice_fusion.3
  565.8 1.0 copy-done
  566.8 2.7 fusion.55
  569.4 4.0 constant_dynamic-slice_fusion.3
  575.3 1.0 copy-done
  576.3 2.7 fusion.55
  578.9 4.0 constant_dynamic-slice_fusion.3
  584.8 1.0 copy-done
  585.8 2.7 fusion.55
  588.5 4.0 constant_dynamic-slice_fusion.3
  594.3 1.0 copy-done
  595.3 2.7 fusion.55
  598.0 4.0 constant_dynamic-slice_fusion.3
  603.8 1.0 copy-done
  604.8 2.7 fusion.55
  607.5 4.0 constant_dynamic-slice_fusion.3
  613.3 1.0 copy-done
  614.3 2.7 fusion.55
  617.0 4.0 constant_dynamic-slice_fusion.3
  622.8 1.0 copy-done
  623.8 2.7 fusion.55
  626.9 1.9 fusion.19
  628.9 7.2 %all_to_all.69 = bf16[4,16,1024]{2,1,0:T(8,128)(2,1)S(1)} all-to-all(bf16[4,16,1024]{2,1,0:T(8,128)(2,1)S(1)} %convert_element_type.51), channel_id=1, replica_groups=mesh['ctx'=8,'uly'=4] {'uly'}, dimensions={0} | all-to-all | bytes 262144 | tf_op jit(solution)/shard_map/all_to_all | solution.py:135
  636.5 1.9 collective-permute-start
  639.9 4.0 collective-permute-done
  644.0 0.9 fusion.28
  (112 shorter events, 16.9 us)
Async XLA Ops:
  6.5 48.2 %all-gather.9.cloned.1.call-start = ((), (), s32[]{:S(2)}) async-start(), calls=%async_computation.6 | async-start | bytes 1179648 | tf_op jit(solution)/shard_map/all_gather | solution.py:126
  15.2 80.7 %all-gather.11.cloned.1.call-start = ((), (), s32[]{:S(2)}) async-start(), calls=%async_computation.7 | async-start | bytes 1179648 | tf_op jit(solution)/shard_map/all_gather | solution.py:127
  23.8 299.7 %all-gather.5.cloned.1.call-start = ((), (), s32[]{:S(2)}) async-start(), calls=%async_computation.4 | async-start | bytes 18874368 | tf_op jit(solution)/shard_map/all_gather | solution.py:119
  27.8 1.6 copy-start.1
  27.9 523.5 %all-gather.7.cloned.1.call-start = ((), (), s32[]{:S(2)}) async-start(), calls=%async_computation.5 | async-start | bytes 18874368 | tf_op jit(solution)/shard_map/all_gather | solution.py:120
  32.0 0.9 copy-start.4
  33.6 7.9 %all-to-all-start = ((bf16[16,4,1024]{2,0,1:T(8,128)(2,1)}), bf16[16,4,1024]{2,0,1:T(8,128)(2,1)S(1)}, u32[]{:S(2)}, u32[]{:S(2)}) async-start(bf16[16,4,1024]{2,0,1:T(8,128)(2,1)} %bitcast.78), calls=%async_computation | async-start | bytes 262144 | tf_op jit(solution)/shard_map/all_to_all | solution.py:108
  556.6 1.6 copy-start
  565.2 1.6 copy-start
  574.7 1.6 copy-start
  584.2 1.6 copy-start
  593.7 1.6 copy-start
  603.2 1.6 copy-start
  612.7 1.6 copy-start
  622.2 1.6 copy-start
  626.9 9.5 %copy-start.2 = (bf16[16,4096]{1,0:T(8,128)(2,1)S(1)}, bf16[16,4096]{1,0:T(8,128)(2,1)}, u32[]{:S(2)}) copy-start(bf16[16,4096]{1,0:T(8,128)(2,1)} %param.21) | copy-start | bytes 393220
  626.9 9.5 %copy-start.7 = (f32[4096]{0:T(1024)S(1)}, f32[4096]{0:T(1024)}, u32[]{:S(2)}) copy-start(f32[4096]{0:T(1024)} %param.20) | copy-start | bytes 49156
  626.9 11.6 %copy-start.8 = (f32[7,256]{1,0:T(8,128)S(1)}, f32[7,256]{1,0:T(8,128)}, u32[]{:S(2)}) copy-start(f32[7,256]{1,0:T(8,128)} %param.24) | copy-start | bytes 21508
  628.9 15.0 %copy-start.5 = (bf16[6,4096]{1,0:T(8,128)(2,1)S(1)}, bf16[6,4096]{1,0:T(8,128)(2,1)}, u32[]{:S(2)}) copy-start(bf16[6,4096]{1,0:T(8,128)(2,1)} %param.23) | copy-start | bytes 147460
  636.2 7.8 %copy-start.3 = (bf16[16,4096]{1,0:T(8,128)(2,1)S(1)}, bf16[16,4096]{1,0:T(8,128)(2,1)}, u32[]{:S(2)}) copy-start(bf16[16,4096]{1,0:T(8,128)(2,1)} %param.22) | copy-start | bytes 393220
  636.2 7.8 %copy-start.6 = (f32[4096]{0:T(1024)S(1)}, f32[4096]{0:T(1024)}, u32[]{:S(2)}) copy-start(f32[4096]{0:T(1024)} %param.25) | copy-start | bytes 49156
  636.5 7.4 %collective-permute-start = (bf16[6,4096]{1,0:T(8,128)(2,1)S(1)}, bf16[6,4096]{1,0:T(8,128)(2,1)S(1)}, u32[]{:S(2)}, u32[]{:S(2)}) collective-permute-start(bf16[6,4096]{1,0:T(8,128)(2,1)S(1)} %slice.95), channel_id=1, source_target_pairs={{0,1},{1,2},{2,3},{3,4},{4,5},{5,6},{6,7},{7,8},{8,9},{9,10},{10,1... | collective-permute-start | bytes 147464 | tf_op jit(solution)/shard_map/ppermute | solution.py:14
Sparse Core Ops, SparseCore 0:
  15.3 39.4 all-gather.8
  56.9 38.8 all-gather.10
  98.0 225.4 all-gather.4
  325.6 225.7 all-gather.6
where the time goes:
time: 653 us; the launch traced here: 651 us
  waiting for transfers between devices  514 us (79%)
  local copies, waits for them, and re-layouts  56.7 us (9%)
  matrix products  27.4 us (4%)
  blocking collectives  22.5 us (3%)
  between operations  13.5 us (2%)
  other arithmetic  11.4 us (2%)
    all_gather x1, waiting for transfers between devices, body(): lax.all_gather(cache_v, 'ctx', axis=0, tiled=True)  228 us
    all_gather x1, waiting for transfers between devices, body(): lax.all_gather(cache_k, 'ctx', axis=0, tiled=True)  225 us
    all_gather x1, waiting for transfers between devices, body(): lax.all_gather(values_here, 'ctx', axis=0, tiled=True)  39.6 us
    dynamic_slice x8, local copies, waits for them, and re-layouts, advance(): lax.dynamic_slice_in_dim(value_rows, offset, block_width, 0)  31.8 us
    dot_general x9, matrix products, online(): jnp.einsum('qhk,khd->qhd', weights.astype(jnp.bfloat16), value_heads, pre...  22.2 us
    all_gather x1, waiting for transfers between devices, body(): lax.all_gather(keys_here, 'ctx', axis=0, tiled=True)  13.2 us
  transfers between devices with their start and end apart: 6, of which 6 were waited for; matrix products, arithmetic and copies ran while one was open for 2% of the time, Pallas kernels for 0%

commit v1 on v0

v1 whole, which is shorter than its diff:
```python
import functools
import math

import jax
import jax.numpy as jnp
from jax import lax
from jax.experimental import pallas as pl
from jax.experimental.pallas import tpu as pltpu
from jax.sharding import PartitionSpec as P

DH = 128
MASKED = -(2.0**100)
EXP2_SCALE = math.log2(math.e) / math.sqrt(DH)
VMEM = pl.BlockSpec(memory_space=pltpu.VMEM)
SMEM = pl.BlockSpec(memory_space=pltpu.SMEM)
PARAMS = pltpu.CompilerParams(vmem_limit_bytes=40 * 2**20)


def swap(block, axis, distance):
    return lax.ppermute(
        block, axis, [(i, i ^ distance) for i in range(lax.axis_size(axis))]
    )


def attend_kernel(starts, limit, newpos, q, k, v, k_new, v_new, out, *, rows_each):
    rows, slots, fresh = q.shape[0], k.shape[0], k_new.shape[0]
    heads = q.shape[1] // DH
    bias = jnp.where(
        lax.broadcasted_iota(jnp.int32, (1, slots), 1) < limit[0], 0.0, MASKED
    ).astype(jnp.float32)
    in_block = lax.broadcasted_iota(jnp.int32, (rows_each, fresh), 0)
    positions = jnp.concatenate(
        [in_block + starts[b] for b in range(rows // rows_each)], axis=0
    )
    visible = newpos[...] <= positions
    lane = lax.broadcasted_iota(jnp.int32, (rows, DH), 1)
    stats = jnp.zeros((rows, DH), jnp.float32)
    ones = jnp.ones((slots, DH), jnp.bfloat16)
    ones_new = jnp.ones((fresh, DH), jnp.bfloat16)
    across = (((1,), (1,)), ((), ()))
    for h in range(heads):
        cols = slice(h * DH, (h + 1) * DH)
        queries = q[:, cols]
        scores = lax.dot_general(queries, k[:, cols], across, preferred_element_type=jnp.float32)
        scores = scores + bias
        scores_new = lax.dot_general(
            queries, k_new[:, cols], across, preferred_element_type=jnp.float32
        )
        scores_new = jnp.where(visible, scores_new, MASKED)
        top = jnp.maximum(
            jnp.max(scores, axis=1, keepdims=True), jnp.max(scores_new, axis=1, keepdims=True)
        )
        top = top.astype(jnp.bfloat16).astype(jnp.float32)
        weights = jnp.exp2((scores - top) * EXP2_SCALE).astype(jnp.bfloat16)
        weights_new = jnp.exp2((scores_new - top) * EXP2_SCALE).astype(jnp.bfloat16)
        both = jnp.dot(
            weights,
            jnp.concatenate([v[:, cols], ones], axis=1),
            preferred_element_type=jnp.float32,
        ) + jnp.dot(
            weights_new,
            jnp.concatenate([v_new[:, cols], ones_new], axis=1),
            preferred_element_type=jnp.float32,
        )
        out[:, cols] = both[:, :DH].astype(jnp.bfloat16)
        total = both[:, DH:]
        coarse = total.astype(jnp.bfloat16).astype(jnp.float32)
        stats = jnp.where(lane == h, top, stats)
        stats = jnp.where(lane == heads + h, coarse, stats)
        stats = jnp.where(lane == 2 * heads + h, total - coarse, stats)
    out[:, heads * DH :] = stats.astype(jnp.bfloat16)


def attend(starts, limit, newpos, q, k, v, k_new, v_new, rows_each):
    rows, width = q.shape
    keys = k.shape[0] + k_new.shape[0]
    return pl.pallas_call(
        functools.partial(attend_kernel, rows_each=rows_each),
        out_shape=jax.ShapeDtypeStruct((rows, width + DH), jnp.bfloat16),
        in_specs=[SMEM, SMEM] + [VMEM] * 6,
        out_specs=VMEM,
        compiler_params=PARAMS,
        cost_estimate=pl.CostEstimate(
            flops=4 * rows * keys * width,
            bytes_accessed=4 * keys * width + 4 * rows * width,
            transcendentals=rows * keys * width // DH,
        ),
        name="attend",
    )(starts, limit, newpos, q, k, v, k_new, v_new)


def combine_kernel(*refs, final):
    parts, out = refs[:-1], refs[-1]
    rows, heads = out.shape[0], (parts[0].shape[1] - DH) // DH
    stats = [p[:, heads * DH :].astype(jnp.float32) for p in parts]
    top = functools.reduce(jnp.maximum, [s[:, :heads] for s in stats])
    factors = [jnp.exp2((s[:, :heads] - top) * EXP2_SCALE) for s in stats]
    total = sum(
        f * (s[:, heads : 2 * heads] + s[:, 2 * heads : 3 * heads])
        for f, s in zip(factors, stats)
    )
    if final:
        factors = [f / total for f in factors]
    for h in range(heads):
        cols = slice(h * DH, (h + 1) * DH)
        mixed = sum(
            p[:, cols].astype(jnp.float32) * f[:, h : h + 1] for p, f in zip(parts, factors)
        )
        out[:, cols] = mixed.astype(jnp.bfloat16)
    if not final:
        coarse = total.astype(jnp.bfloat16).astype(jnp.float32)
        rest = jnp.zeros((rows, DH - 3 * heads), jnp.float32)
        out[:, heads * DH :] = jnp.concatenate(
            [top, coarse, total - coarse, rest], axis=1
        ).astype(jnp.bfloat16)


def combine(parts, final):
    rows, width = parts[0].shape
    out_width = width - DH if final else width
    return pl.pallas_call(
        functools.partial(combine_kernel, final=final),
        out_shape=jax.ShapeDtypeStruct((rows, out_width), jnp.bfloat16),
        in_specs=[VMEM] * len(parts),
        out_specs=VMEM,
        compiler_params=PARAMS,
        cost_estimate=pl.CostEstimate(
            flops=4 * len(parts) * rows * width,
            bytes_accessed=2 * (len(parts) + 1) * rows * width,
            transcendentals=rows * 8,
        ),
        name="combine",
    )(*parts)


def body(
    q_new,
    k_new,
    v_new,
    cache_k,
    cache_v,
    filled_slots,
    norm_gain,
    v_branch,
    x_gate,
    conv_state,
    conv_filter,
    skip_gain,
):
    ctx_size, uly_size = lax.axis_size("ctx"), lax.axis_size("uly")
    ctx, uly = lax.axis_index("ctx"), lax.axis_index("uly")
    tokens = q_new.shape[0]
    slots = cache_k.shape[0]
    bits = [1 << b for b in reversed(range(uly_size.bit_length() - 1))]

    def to_heads(block):
        for bit in bits:
            half = block.shape[1] // 2
            left, right = block[:, :half], block[:, half:]
            low = (uly & bit) == 0
            kept, sent = jnp.where(low, left, right), jnp.where(low, right, left)
            block = jnp.concatenate([kept, swap(sent, "uly", bit)], axis=0)
        return block

    def to_tokens(block):
        for bit in reversed(bits):
            half = block.shape[0] // 2
            kept, received = block[:half], swap(block[half:], "uly", bit)
            low = (uly & bit) == 0
            block = jnp.concatenate(
                [jnp.where(low, kept, received), jnp.where(low, received, kept)], axis=1
            )
        return block

    offsets = [0]
    for bit in bits:
        offsets = offsets + [o | bit for o in offsets]
    owners = uly ^ jnp.array(offsets, jnp.int32)

    def starts_of(distance):
        return ((ctx ^ distance) * uly_size + owners) * tokens

    limit = jnp.clip(filled_slots - ctx * slots, 0, slots).astype(jnp.int32)
    newpos = (starts_of(0)[:, None] + jnp.arange(tokens, dtype=jnp.int32)[None, :]).reshape(1, -1)

    here = to_heads(q_new)
    fresh = to_heads(jnp.concatenate([k_new, v_new], axis=0))
    fresh = fresh.reshape(uly_size, 2, tokens, -1)
    fresh_k = fresh[:, 0].reshape(here.shape)
    fresh_v = fresh[:, 1].reshape(here.shape)

    distances = list(range(2, ctx_size, 2))[::-1] + [0]
    mine = [swap(here, "ctx", d) if d else here for d in distances]
    other = [swap(block, "ctx", 1) for block in mine]

    def run(blocks, block_distances):
        starts = jnp.concatenate([starts_of(d) for d in block_distances])
        return attend(
            starts,
            limit,
            newpos,
            jnp.concatenate(blocks, axis=0),
            cache_k,
            cache_v,
            fresh_k,
            fresh_v,
            tokens,
        )

    rows = here.shape[0]
    other_distances = [d ^ 1 for d in distances]
    half = len(distances) // 2
    out_mine = run(mine, distances)
    returned = []
    for part in (slice(0, half), slice(half, None)):
        out_other = run(other[part], other_distances[part])
        back = swap(out_other, "ctx", 1)
        first = part.start * rows
        merged = combine([out_mine[first : first + back.shape[0]], back], False)
        for i, d in enumerate(distances[part]):
            piece = merged[i * rows : (i + 1) * rows]
            returned.append(swap(piece, "ctx", d) if d else piece)
    attended = combine(returned, True)
    token_rows = to_tokens(attended)

    values32 = token_rows.astype(jnp.float32)
    normed = (
        values32
        * lax.rsqrt(jnp.mean(values32 * values32, axis=1, keepdims=True) + 1e-06)
        * norm_gain
    )
    conv_input = lax.optimization_barrier(
        (normed * v_branch.astype(jnp.float32)).astype(jnp.bfloat16)
    )
    conv_reach = conv_filter.shape[0] - 1
    axes = ("ctx", "uly")
    count = ctx_size * uly_size
    incoming = lax.ppermute(conv_input[-conv_reach:], axes, [(i, i + 1) for i in range(count - 1)])
    first_device = jnp.logical_and(ctx == 0, uly == 0)
    lower_rim = jnp.where(first_device, conv_state, incoming)
    extended = jnp.concatenate([lower_rim, conv_input], axis=0).astype(jnp.float32)
    tap_table = jnp.repeat(conv_filter, conv_input.shape[1] // conv_filter.shape[1], axis=1)
    filtered = tap_table[0] * extended[conv_reach : conv_reach + tokens]
    for lag in range(1, conv_reach + 1):
        filtered = filtered + tap_table[lag] * extended[conv_reach - lag : conv_reach - lag + tokens]
    result = x_gate.astype(jnp.float32) * (filtered + skip_gain * conv_input.astype(jnp.float32))
    return result.astype(jnp.bfloat16)


def solution(mesh):
    split = P(("ctx", "uly"), None)
    in_specs = (
        split, split, split, P("ctx", "uly"), P("ctx", "uly"), P(),
        P(), split, split, P(), P(), P(),
    )
    return jax.shard_map(body, mesh=mesh, in_specs=in_specs, out_specs=split, check_vma=False)
```

time: 653 us -> 69.2 us (0.11)
  waiting for transfers between devices: 514 us -> 26.6 us
  local copies, waits for them, and re-layouts: 56.7 us -> 3.48 us
  matrix products: 27.4 us -> 0 us
  blocking collectives: 22.5 us -> 0 us
  starting transfers between devices: 5.37 us -> 22.4 us
  between operations: 13.5 us -> 1.14 us
  Pallas kernels: 0 us -> 12.1 us
  other arithmetic: 11.4 us -> 3.32 us
    all_gather x4 -> x0, waiting for transfers between devices: 506 us -> none  [the longest x1 228 us: body(): lax.all_gather(cache_v, 'ctx', axis=0, tiled=True)]
    dynamic_slice x8 -> x0, local copies, waits for them, and re-layouts: 31.8 us -> none  [advance(): lax.dynamic_slice_in_dim(value_rows, offset, block_width, 0)]
    dot_general x18 -> x0, matrix products: 27.4 us -> none  [the longest x9 22.2 us: online(): jnp.einsum('qhk,khd->qhd', weights.astype(jnp.bfloat16), value_heads, pre...]
    ppermute x1 -> x19, waiting for transfers between devices: 3.97 us -> 26.6 us  [the longest x18 22.6 us: swap(): lax.ppermute(block, axis, [(i, i ^ distance) for i in range(lax.axis_size...]
    all_to_all x3 -> x0, blocking collectives: 22.5 us -> none  [the longest x1 7.68 us: body(): lax.all_to_all(k_new, 'uly', split_axis=1, concat_axis=0, tiled=True)]
    ppermute x1 -> x19, starting transfers between devices: 1.92 us -> 22.4 us  [the longest x18 20.5 us: swap(): lax.ppermute(block, axis, [(i, i ^ distance) for i in range(lax.axis_size...]
    pallas_call x0 -> x6, Pallas kernels: none -> 12.1 us  [the longest x3 10.6 us: attend(): pl.pallas_call(functools.partial(attend_kernel, rows_each=rows_each), out...]
    while x24 -> x0, local copies, waits for them, and re-layouts: 8.04 us -> none
  transfers between devices with their start and end apart: 6 -> 19, of which waited for: 6 -> 11; matrix products, arithmetic and copies ran while one was open for 2% -> 7% of each run, Pallas kernels for 0% -> 17%
where the time goes in v1:
time: 69.2 us; the launch traced here: 69 us
  waiting for transfers between devices  26.6 us (38%)
  starting transfers between devices  22.4 us (32%)
  Pallas kernels  12.1 us (17%)
  local copies, waits for them, and re-layouts  3.48 us (5%)
  other arithmetic  3.32 us (5%)
  between operations  1.14 us (2%)
    ppermute x18, waiting for transfers between devices, swap(): lax.ppermute(block, axis, [(i, i ^ distance) for i in range(lax.axis_size...  22.6 us
    ppermute x18, starting transfers between devices, swap(): lax.ppermute(block, axis, [(i, i ^ distance) for i in range(lax.axis_size...  20.5 us
    pallas_call x3, Pallas kernels, attend(): pl.pallas_call(functools.partial(attend_kernel, rows_each=rows_each), out...  10.6 us
    ppermute x1, waiting for transfers between devices, body(): lax.ppermute(conv_input[-conv_reach:], axes, [(i, i + 1) for i in range(c...  3.97 us
    ppermute x1, starting transfers between devices, body(): lax.ppermute(conv_input[-conv_reach:], axes, [(i, i + 1) for i in range(c...  1.92 us
    pallas_call x3, Pallas kernels, combine(): pl.pallas_call(functools.partial(combine_kernel, final=final), out_shape=...  1.43 us
  transfers between devices with their start and end apart: 19, of which 11 were waited for; matrix products, arithmetic and copies ran while one was open for 7% of the time, Pallas kernels for 17%

profile of v1, /device:TPU:8, one launch (start us, length us, event | category | flops | bytes accessed | tf_op | source)
XLA Modules:
  0.0 69.0 jit_solution(1605397665844661910)
XLA Ops:
  0.0 0.9 %broadcast_select_fusion.11 = (bf16[16,2048]{1,0:T(8,128)(2,1)S(1)}, bf16[16,2048]{1,0:T(8,128)(2,1)S(1)}) fusion(pred[]{:T(512)S(6)} %eq.18, bf16[16,4096]{1,0:T(8,128)(2,1)} %param.13), kind=kLoop, calls=%fused_computation.51 | loop fusion | flops 65536 | bytes 262145 | tf_op jit(solution)/shard_map/jit(_where)/select_n | solution.py:161
  0.9 1.6 %collective-permute-start = (bf16[16,2048]{1,0:T(8,128)(2,1)S(1)}, bf16[16,2048]{1,0:T(8,128)(2,1)S(1)}, u32[]{:S(2)}, u32[]{:S(2)}) collective-permute-start(bf16[16,2048]{1,0:T(8,128)(2,1)S(1)} %get-tuple-element.24), channel_id=1, source_target_pairs={{0,2},{1,3},{2,0},{3,1},{4,6},{5,7},{6,4},{7,5},{8,10},{9,11},{10,... | collective-permute-start | bytes 196616 | tf_op jit(solution)/shard_map/ppermute | solution.py:20
  2.5 0.9 %constant_dynamic-update-slice_fusion.6 = bf16[32,4096]{1,0:T(8,128)(2,1)S(1)} fusion(bf16[16,4096]{1,0:T(8,128)(2,1)} %param.14), kind=kLoop, calls=%fused_computation.59 | loop fusion | bytes 262144
  3.4 0.9 %constant_dynamic-update-slice_fusion.5 = bf16[32,4096]{1,0:T(8,128)(2,1)S(1)} fusion(bf16[32,4096]{1,0:T(8,128)(2,1)S(1)} %constant_dynamic-update-slice_fusion.6, bf16[16,4096]{1,0:T(8,128)(2,1)} %param.15), kind=kLoop, calls=%fused_computation.58 | loop fusion | bytes 262144 | tf_op jit(solution)/shard_map/concatenate | solution.py:187
  4.4 0.6 collective-permute-start.5
  5.0 0.7 fusion.22
  6.0 1.2 %collective-permute-done.1 = bf16[32,1024]{1,0:T(8,128)(2,1)S(1)} collective-permute-done((bf16[32,1024]{1,0:T(8,128)(2,1)S(1)}, bf16[32,1024]{1,0:T(8,128)(2,1)S(1)}, u32[]{:S(2)}, u32[]{:S(2)}) %collective-permute-start.1) | collective-permute-done | bytes 65568 | tf_op jit(solution)/shard_map/ppermute | solution.py:20
  7.1 1.6 %collective-permute-start.2 = (bf16[64,1024]{1,0:T(8,128)(2,1)S(1)}, bf16[64,1024]{1,0:T(8,128)(2,1)S(1)}, u32[]{:S(2)}, u32[]{:S(2)}) collective-permute-start(bf16[64,1024]{1,0:T(8,128)(2,1)S(1)} %pad_maximum_fusion.4), channel_id=1, source_target_pairs={{0,24},{4,28},{8,16},{12,20},{16,8},{20,12},{24,0},{28,4},{1,25},{... | collective-permute-start | bytes 393224 | tf_op jit(solution)/shard_map/ppermute | solution.py:20
  9.6 1.0 %collective-permute-start.3 = (bf16[64,1024]{1,0:T(8,128)(2,1)S(1)}, bf16[64,1024]{1,0:T(8,128)(2,1)S(1)}, u32[]{:S(2)}, u32[]{:S(2)}) collective-permute-start(bf16[64,1024]{1,0:T(8,128)(2,1)S(1)} %pad_maximum_fusion.4), channel_id=1, source_target_pairs={{0,16},{4,20},{8,24},{12,28},{16,0},{20,4},{24,8},{28,12},{1,17},{... | collective-permute-start | bytes 393224 | tf_op jit(solution)/shard_map/ppermute | solution.py:20
  10.7 1.5 %collective-permute-start.4 = (bf16[64,1024]{1,0:T(8,128)(2,1)S(1)}, bf16[64,1024]{1,0:T(8,128)(2,1)S(1)}, u32[]{:S(2)}, u32[]{:S(2)}) collective-permute-start(bf16[64,1024]{1,0:T(8,128)(2,1)S(1)} %pad_maximum_fusion.4), channel_id=1, source_target_pairs={{0,8},{4,12},{8,0},{12,4},{16,24},{20,28},{24,16},{28,20},{1,9},{5... | collective-permute-start | bytes 393224 | tf_op jit(solution)/shard_map/ppermute | solution.py:20
  12.2 1.5 %collective-permute-start.13 = (bf16[64,1024]{1,0:T(8,128)(2,1)S(1)}, bf16[64,1024]{1,0:T(8,128)(2,1)S(1)}, u32[]{:S(2)}, u32[]{:S(2)}) collective-permute-start(bf16[64,1024]{1,0:T(8,128)(2,1)S(1)} %pad_maximum_fusion.4), channel_id=1, source_target_pairs={{0,4},{4,0},{8,12},{12,8},{16,20},{20,16},{24,28},{28,24},{1,5},{5... | collective-permute-start | bytes 393224 | tf_op jit(solution)/shard_map/ppermute | solution.py:20
  13.8 5.4 %collective-permute-done.2 = bf16[64,1024]{1,0:T(8,128)(2,1)S(1)} collective-permute-done((bf16[64,1024]{1,0:T(8,128)(2,1)S(1)}, bf16[64,1024]{1,0:T(8,128)(2,1)S(1)}, u32[]{:S(2)}, u32[]{:S(2)}) %collective-permute-start.2) | collective-permute-done | bytes 131104 | tf_op jit(solution)/shard_map/ppermute | solution.py:20
  19.2 1.1 %collective-permute-done.3 = bf16[64,1024]{1,0:T(8,128)(2,1)S(1)} collective-permute-done((bf16[64,1024]{1,0:T(8,128)(2,1)S(1)}, bf16[64,1024]{1,0:T(8,128)(2,1)S(1)}, u32[]{:S(2)}, u32[]{:S(2)}) %collective-permute-start.3) | collective-permute-done | bytes 131104 | tf_op jit(solution)/shard_map/ppermute | solution.py:20
  20.3 0.2 collective-permute-done.4
  20.6 1.6 %collective-permute-start.8 = (bf16[64,1024]{1,0:T(8,128)(2,1)S(1)}, bf16[64,1024]{1,0:T(8,128)(2,1)S(1)}, u32[]{:S(2)}, u32[]{:S(2)}) collective-permute-start(bf16[64,1024]{1,0:T(8,128)(2,1)S(1)} %collective-permute-done.3), channel_id=1, source_target_pairs={{0,4},{4,0},{8,12},{12,8},{16,20},{20,16},{24,28},{28,24},{1,5},{5... | collective-permute-start | bytes 393224 | tf_op jit(solution)/shard_map/ppermute | solution.py:20
  22.1 0.5 collective-permute-start.7
  22.6 1.5 %collective-permute-start.12 = (bf16[64,1024]{1,0:T(8,128)(2,1)S(1)}, bf16[64,1024]{1,0:T(8,128)(2,1)S(1)}, u32[]{:S(2)}, u32[]{:S(2)}) collective-permute-start(bf16[64,1024]{1,0:T(8,128)(2,1)S(1)} %collective-permute-done.4), channel_id=1, source_target_pairs={{0,4},{4,0},{8,12},{12,8},{16,20},{20,16},{24,28},{28,24},{1,5},{5... | collective-permute-start | bytes 393224 | tf_op jit(solution)/shard_map/ppermute | solution.py:20
  24.2 4.8 %attend.3 = bf16[256,1152]{1,0:T(8,128)(2,1)S(1)} custom-call(s32[16]{0:T(128)S(1)} %pad_add_fusion.starts, s32[1]{0:T(128)S(6)} %min.6.limit, s32[1,64]{1,0:T(1,128)S(1)} %add.113.newpos, bf16[256,1024]{1,0:T(8,128)(2,1)S(1)} %constant_dynamic-update-slice_fusion.q, bf16[1024,1024]{1,0:T(8,128)(2,1)S(1)} %copy-done, bf16[1024,1024]{1,0:T(8,128)(2,1)S(1)} %copy-done.1, ...), custom_call_target="tpu_custom_call" | custom-call | flops 1140850688 | bytes 5505024 | tf_op jit(solution)/shard_map/attend/pallas_call | solution.py:77
  29.0 0.6 collective-permute-done.7
  29.6 2.9 %attend.4 = bf16[128,1152]{1,0:T(8,128)(2,1)S(1)} custom-call(s32[8]{0:T(128)S(1)} %pad_add_fusion.1.starts, s32[1]{0:T(128)S(6)} %min.6.limit, s32[1,64]{1,0:T(1,128)S(1)} %add.113.newpos, bf16[128,1024]{1,0:T(8,128)(2,1)S(1)} %pad_maximum_fusion.1.q, bf16[1024,1024]{1,0:T(8,128)(2,1)S(1)} %copy-done, bf16[1024,1024]{1,0:T(8,128)(2,1)S(1)} %copy-done.1, ...), custom_call_target="tpu_custom_call" | custom-call | flops 570425344 | bytes 4980736 | tf_op jit(solution)/shard_map/attend/pallas_call | solution.py:77
  32.5 1.6 %collective-permute-start.9 = (bf16[128,1152]{1,0:T(8,128)(2,1)S(1)}, bf16[128,1152]{1,0:T(8,128)(2,1)S(1)}, u32[]{:S(2)}, u32[]{:S(2)}) collective-permute-start(bf16[128,1152]{1,0:T(8,128)(2,1)S(1)} %attend.4), channel_id=1, source_target_pairs={{0,4},{4,0},{8,12},{12,8},{16,20},{20,16},{24,28},{28,24},{1,5},{5... | collective-permute-start | bytes 884744 | tf_op jit(solution)/shard_map/ppermute | solution.py:20
  34.2 2.9 %attend.5 = bf16[128,1152]{1,0:T(8,128)(2,1)S(1)} custom-call(s32[8]{0:T(128)S(1)} %pad_add_fusion.2.starts, s32[1]{0:T(128)S(6)} %min.6.limit, s32[1,64]{1,0:T(1,128)S(1)} %add.113.newpos, bf16[128,1024]{1,0:T(8,128)(2,1)S(1)} %pad_maximum_fusion.2.q, bf16[1024,1024]{1,0:T(8,128)(2,1)S(1)} %copy-done, bf16[1024,1024]{1,0:T(8,128)(2,1)S(1)} %copy-done.1, ...), custom_call_target="tpu_custom_call" | custom-call | flops 570425344 | bytes 4980736 | tf_op jit(solution)/shard_map/attend/pallas_call | solution.py:77
  37.1 0.6 collective-permute-start.14
  37.7 4.7 %collective-permute-done.9.refs_1_ = bf16[128,1152]{1,0:T(8,128)(2,1)S(1)} collective-permute-done((bf16[128,1152]{1,0:T(8,128)(2,1)S(1)}, bf16[128,1152]{1,0:T(8,128)(2,1)S(1)}, u32[]{:S(2)}, u32[]{:S(2)}) %collective-permute-start.9) | collective-permute-done | bytes 294944 | tf_op jit(solution)/shard_map/ppermute | solution.py:20
  42.4 0.5 combine.3
  42.9 0.4 collective-permute-start.10
  43.3 4.2 %collective-permute-start.11 = (bf16[64,1152]{1,0:T(8,128)(2,1)S(1)}, bf16[64,1152]{1,0:T(8,128)(2,1)S(1)}, u32[]{:S(2)}, u32[]{:S(2)}) collective-permute-start(bf16[64,1152]{1,0:T(8,128)(2,1)S(1)} %get-tuple-element.9), channel_id=1, source_target_pairs={{0,16},{4,20},{8,24},{12,28},{16,0},{20,4},{24,8},{28,12},{1,17},{... | collective-permute-start | bytes 442376 | tf_op jit(solution)/shard_map/ppermute | solution.py:20
  47.5 0.5 combine.4
  48.0 0.5 collective-permute-start.15
  48.5 4.4 %collective-permute-done.11.refs_1_ = bf16[64,1152]{1,0:T(8,128)(2,1)S(1)} collective-permute-done((bf16[64,1152]{1,0:T(8,128)(2,1)S(1)}, bf16[64,1152]{1,0:T(8,128)(2,1)S(1)}, u32[]{:S(2)}, u32[]{:S(2)}) %collective-permute-start.11) | collective-permute-done | bytes 147488 | tf_op jit(solution)/shard_map/ppermute | solution.py:20
  53.0 1.1 %collective-permute-done.15.refs_2_ = bf16[64,1152]{1,0:T(8,128)(2,1)S(1)} collective-permute-done((bf16[64,1152]{1,0:T(8,128)(2,1)S(1)}, bf16[64,1152]{1,0:T(8,128)(2,1)S(1)}, u32[]{:S(2)}, u32[]{:S(2)}) %collective-permute-start.15) | collective-permute-done | bytes 147488 | tf_op jit(solution)/shard_map/ppermute | solution.py:20
  54.0 0.5 combine.5
  54.7 1.2 %collective-permute-done.16 = bf16[32,1024]{1,0:T(8,128)(2,1)S(1)} collective-permute-done((bf16[32,1024]{1,0:T(8,128)(2,1)S(1)}, bf16[32,1024]{1,0:T(8,128)(2,1)S(1)}, u32[]{:S(2)}, u32[]{:S(2)}) %collective-permute-start.16) | collective-permute-done | bytes 65568 | tf_op jit(solution)/shard_map/ppermute | solution.py:20
  55.9 1.5 %collective-permute-start.17 = (bf16[16,2048]{1,0:T(8,128)(2,1)S(1)}, bf16[16,2048]{1,0:T(8,128)(2,1)S(1)}, u32[]{:S(2)}, u32[]{:S(2)}) collective-permute-start(bf16[16,2048]{1,0:T(8,128)(2,1)S(1)} %pad_maximum_fusion.6), channel_id=1, source_target_pairs={{0,2},{1,3},{2,0},{3,1},{4,6},{5,7},{6,4},{7,5},{8,10},{9,11},{10,... | collective-permute-start | bytes 196616 | tf_op jit(solution)/shard_map/ppermute | solution.py:20
  57.5 2.8 %collective-permute-done.17 = bf16[16,2048]{1,0:T(8,128)(2,1)S(1)} collective-permute-done((bf16[16,2048]{1,0:T(8,128)(2,1)S(1)}, bf16[16,2048]{1,0:T(8,128)(2,1)S(1)}, u32[]{:S(2)}, u32[]{:S(2)}) %collective-permute-start.17) | collective-permute-done | bytes 65568 | tf_op jit(solution)/shard_map/ppermute | solution.py:20
  60.3 0.1 fusion
  60.5 0.1 fusion.3
  60.6 1.9 %collective-permute-start.18 = (bf16[6,4096]{1,0:T(8,128)(2,1)S(1)}, bf16[6,4096]{1,0:T(8,128)(2,1)S(1)}, u32[]{:S(2)}, u32[]{:S(2)}) collective-permute-start(bf16[6,4096]{1,0:T(8,128)(2,1)S(1)} %slice.193), channel_id=1, source_target_pairs={{0,1},{1,2},{2,3},{3,4},{4,5},{5,6},{6,7},{7,8},{8,9},{9,10},{10,1... | collective-permute-start | bytes 147464 | tf_op jit(solution)/shard_map/ppermute | solution.py:238
  62.6 0.1 broadcast_in_dim.46
  62.7 0.1 broadcast_in_dim.47
  62.9 0.1 broadcast_in_dim.45
  63.1 0.1 broadcast_in_dim.43
  63.3 0.1 broadcast_in_dim.41
  63.5 0.1 broadcast_in_dim.39
  63.7 0.1 broadcast_in_dim.37
  63.9 0.1 broadcast_in_dim.35
  64.0 4.0 %collective-permute-done.18 = bf16[6,4096]{1,0:T(8,128)(2,1)S(1)} collective-permute-done((bf16[6,4096]{1,0:T(8,128)(2,1)S(1)}, bf16[6,4096]{1,0:T(8,128)(2,1)S(1)}, u32[]{:S(2)}, u32[]{:S(2)}) %collective-permute-start.18) | collective-permute-done | bytes 49184 | tf_op jit(solution)/shard_map/ppermute | solution.py:238
  68.1 0.9 %fusion.7 = bf16[16,4096]{1,0:T(8,128)(2,1)} fusion(f32[22,4096]{1,0:T(8,128)S(1)} %maximum_convert_fusion, bf16[16,4096]{1,0:T(8,128)(2,1)S(1)} %fusion.3, bf16[16,4096]{1,0:T(8,128)(2,1)S(1)} %copy-done.2, f32[4096]{0:T(1024)S(1)} %copy-done.5, f32[4096]{0:T(1024)S(1)} %broadcast_in_dim.47, f32[4096]{0:T(1024)S(1)} %broadcast_in_dim.45, ...), kind=kLoop, calls=%fused_computation.10 | loop fusion | flops 1245184 | bytes 2359296 | tf_op jit(solution)/shard_map/convert_element_type | solution.py:247
  (63 shorter events, 1.7 us)
Async XLA Ops:
  0.9 23.3 %copy-start = (bf16[1024,1024]{1,0:T(8,128)(2,1)S(1)}, bf16[1024,1024]{1,0:T(8,128)(2,1)}, u32[]{:S(2)}) copy-start(bf16[1024,1024]{1,0:T(8,128)(2,1)} %k.5) | copy-start | bytes 6291460
  0.9 4.9 %collective-permute-start = (bf16[16,2048]{1,0:T(8,128)(2,1)S(1)}, bf16[16,2048]{1,0:T(8,128)(2,1)S(1)}, u32[]{:S(2)}, u32[]{:S(2)}) collective-permute-start(bf16[16,2048]{1,0:T(8,128)(2,1)S(1)} %get-tuple-element.24), channel_id=1, source_target_pairs={{0,2},{1,3},{2,0},{3,1},{4,6},{5,7},{6,4},{7,5},{8,10},{9,11},{10,... | collective-permute-start | bytes 196616 | tf_op jit(solution)/shard_map/ppermute | solution.py:20
  4.4 9.3 %collective-permute-start.5 = (bf16[32,2048]{1,0:T(8,128)(2,1)S(1)}, bf16[32,2048]{1,0:T(8,128)(2,1)S(1)}, u32[]{:S(2)}, u32[]{:S(2)}) collective-permute-start(bf16[32,2048]{1,0:T(8,128)(2,1)S(1)} %get-tuple-element.16), channel_id=1, source_target_pairs={{0,2},{1,3},{2,0},{3,1},{4,6},{5,7},{6,4},{7,5},{8,10},{9,11},{10,... | collective-permute-start | bytes 393224 | tf_op jit(solution)/shard_map/ppermute | solution.py:20
  5.8 1.3 %collective-permute-start.1 = (bf16[32,1024]{1,0:T(8,128)(2,1)S(1)}, bf16[32,1024]{1,0:T(8,128)(2,1)S(1)}, u32[]{:S(2)}, u32[]{:S(2)}) collective-permute-start(bf16[32,1024]{1,0:T(8,128)(2,1)S(1)} %get-tuple-element.22), channel_id=1, source_target_pairs={{0,1},{1,0},{2,3},{3,2},{4,5},{5,4},{6,7},{7,6},{8,9},{9,8},{10,11... | collective-permute-start | bytes 196616 | tf_op jit(solution)/shard_map/ppermute | solution.py:20
  7.1 12.0 %collective-permute-start.2 = (bf16[64,1024]{1,0:T(8,128)(2,1)S(1)}, bf16[64,1024]{1,0:T(8,128)(2,1)S(1)}, u32[]{:S(2)}, u32[]{:S(2)}) collective-permute-start(bf16[64,1024]{1,0:T(8,128)(2,1)S(1)} %pad_maximum_fusion.4), channel_id=1, source_target_pairs={{0,24},{4,28},{8,16},{12,20},{16,8},{20,12},{24,0},{28,4},{1,25},{... | collective-permute-start | bytes 393224 | tf_op jit(solution)/shard_map/ppermute | solution.py:20
  9.6 14.5 %copy-start.1 = (bf16[1024,1024]{1,0:T(8,128)(2,1)S(1)}, bf16[1024,1024]{1,0:T(8,128)(2,1)}, u32[]{:S(2)}) copy-start(bf16[1024,1024]{1,0:T(8,128)(2,1)} %v.5) | copy-start | bytes 6291460
  9.6 10.7 %collective-permute-start.3 = (bf16[64,1024]{1,0:T(8,128)(2,1)S(1)}, bf16[64,1024]{1,0:T(8,128)(2,1)S(1)}, u32[]{:S(2)}, u32[]{:S(2)}) collective-permute-start(bf16[64,1024]{1,0:T(8,128)(2,1)S(1)} %pad_maximum_fusion.4), channel_id=1, source_target_pairs={{0,16},{4,20},{8,24},{12,28},{16,0},{20,4},{24,8},{28,12},{1,17},{... | collective-permute-start | bytes 393224 | tf_op jit(solution)/shard_map/ppermute | solution.py:20
  10.7 9.8 %collective-permute-start.4 = (bf16[64,1024]{1,0:T(8,128)(2,1)S(1)}, bf16[64,1024]{1,0:T(8,128)(2,1)S(1)}, u32[]{:S(2)}, u32[]{:S(2)}) collective-permute-start(bf16[64,1024]{1,0:T(8,128)(2,1)S(1)} %pad_maximum_fusion.4), channel_id=1, source_target_pairs={{0,8},{4,12},{8,0},{12,4},{16,24},{20,28},{24,16},{28,20},{1,9},{5... | collective-permute-start | bytes 393224 | tf_op jit(solution)/shard_map/ppermute | solution.py:20
  12.2 21.9 %collective-permute-start.13 = (bf16[64,1024]{1,0:T(8,128)(2,1)S(1)}, bf16[64,1024]{1,0:T(8,128)(2,1)S(1)}, u32[]{:S(2)}, u32[]{:S(2)}) collective-permute-start(bf16[64,1024]{1,0:T(8,128)(2,1)S(1)} %pad_maximum_fusion.4), channel_id=1, source_target_pairs={{0,4},{4,0},{8,12},{12,8},{16,20},{20,16},{24,28},{28,24},{1,5},{5... | collective-permute-start | bytes 393224 | tf_op jit(solution)/shard_map/ppermute | solution.py:20
  13.7 6.8 %collective-permute-start.6 = (bf16[64,1024]{1,0:T(8,128)(2,1)S(1)}, bf16[64,1024]{1,0:T(8,128)(2,1)S(1)}, u32[]{:S(2)}, u32[]{:S(2)}) collective-permute-start(bf16[64,1024]{1,0:T(8,128)(2,1)S(1)} %get-tuple-element.14), channel_id=1, source_target_pairs={{0,1},{1,0},{2,3},{3,2},{4,5},{5,4},{6,7},{7,6},{8,9},{9,8},{10,11... | collective-permute-start | bytes 393224 | tf_op jit(solution)/shard_map/ppermute | solution.py:20
  20.6 8.4 %collective-permute-start.8 = (bf16[64,1024]{1,0:T(8,128)(2,1)S(1)}, bf16[64,1024]{1,0:T(8,128)(2,1)S(1)}, u32[]{:S(2)}, u32[]{:S(2)}) collective-permute-start(bf16[64,1024]{1,0:T(8,128)(2,1)S(1)} %collective-permute-done.3), channel_id=1, source_target_pairs={{0,4},{4,0},{8,12},{12,8},{16,20},{20,16},{24,28},{28,24},{1,5},{5... | collective-permute-start | bytes 393224 | tf_op jit(solution)/shard_map/ppermute | solution.py:20
  22.1 7.4 %collective-permute-start.7 = (bf16[64,1024]{1,0:T(8,128)(2,1)S(1)}, bf16[64,1024]{1,0:T(8,128)(2,1)S(1)}, u32[]{:S(2)}, u32[]{:S(2)}) collective-permute-start(bf16[64,1024]{1,0:T(8,128)(2,1)S(1)} %collective-permute-done.2), channel_id=1, source_target_pairs={{0,4},{4,0},{8,12},{12,8},{16,20},{20,16},{24,28},{28,24},{1,5},{5... | collective-permute-start | bytes 393224 | tf_op jit(solution)/shard_map/ppermute | solution.py:20
  22.6 11.5 %collective-permute-start.12 = (bf16[64,1024]{1,0:T(8,128)(2,1)S(1)}, bf16[64,1024]{1,0:T(8,128)(2,1)S(1)}, u32[]{:S(2)}, u32[]{:S(2)}) collective-permute-start(bf16[64,1024]{1,0:T(8,128)(2,1)S(1)} %collective-permute-done.4), channel_id=1, source_target_pairs={{0,4},{4,0},{8,12},{12,8},{16,20},{20,16},{24,28},{28,24},{1,5},{5... | collective-permute-start | bytes 393224 | tf_op jit(solution)/shard_map/ppermute | solution.py:20
  32.5 9.9 %collective-permute-start.9 = (bf16[128,1152]{1,0:T(8,128)(2,1)S(1)}, bf16[128,1152]{1,0:T(8,128)(2,1)S(1)}, u32[]{:S(2)}, u32[]{:S(2)}) collective-permute-start(bf16[128,1152]{1,0:T(8,128)(2,1)S(1)} %attend.4), channel_id=1, source_target_pairs={{0,4},{4,0},{8,12},{12,8},{16,20},{20,16},{24,28},{28,24},{1,5},{5... | collective-permute-start | bytes 884744 | tf_op jit(solution)/shard_map/ppermute | solution.py:20
  37.1 10.5 %collective-permute-start.14 = (bf16[128,1152]{1,0:T(8,128)(2,1)S(1)}, bf16[128,1152]{1,0:T(8,128)(2,1)S(1)}, u32[]{:S(2)}, u32[]{:S(2)}) collective-permute-start(bf16[128,1152]{1,0:T(8,128)(2,1)S(1)} %attend.5), channel_id=1, source_target_pairs={{0,4},{4,0},{8,12},{12,8},{16,20},{20,16},{24,28},{28,24},{1,5},{5... | collective-permute-start | bytes 884744 | tf_op jit(solution)/shard_map/ppermute | solution.py:20
  42.8 17.6 %copy-start.3 = (bf16[16,4096]{1,0:T(8,128)(2,1)S(1)}, bf16[16,4096]{1,0:T(8,128)(2,1)}, u32[]{:S(2)}) copy-start(bf16[16,4096]{1,0:T(8,128)(2,1)} %param.20) | copy-start | bytes 393220
  42.8 17.6 %copy-start.6 = (f32[4096]{0:T(1024)S(1)}, f32[4096]{0:T(1024)}, u32[]{:S(2)}) copy-start(f32[4096]{0:T(1024)} %param.19) | copy-start | bytes 49156
  42.8 19.7 %copy-start.7 = (f32[7,256]{1,0:T(8,128)S(1)}, f32[7,256]{1,0:T(8,128)}, u32[]{:S(2)}) copy-start(f32[7,256]{1,0:T(8,128)} %param.23) | copy-start | bytes 21508
  42.9 5.6 %collective-permute-start.10 = (bf16[64,1152]{1,0:T(8,128)(2,1)S(1)}, bf16[64,1152]{1,0:T(8,128)(2,1)S(1)}, u32[]{:S(2)}, u32[]{:S(2)}) collective-permute-start(bf16[64,1152]{1,0:T(8,128)(2,1)S(1)} %get-tuple-element.10), channel_id=1, source_target_pairs={{0,24},{4,28},{8,16},{12,20},{16,8},{20,12},{24,0},{28,4},{1,25},{... | collective-permute-start | bytes 442376 | tf_op jit(solution)/shard_map/ppermute | solution.py:20
  43.3 9.7 %collective-permute-start.11 = (bf16[64,1152]{1,0:T(8,128)(2,1)S(1)}, bf16[64,1152]{1,0:T(8,128)(2,1)S(1)}, u32[]{:S(2)}, u32[]{:S(2)}) collective-permute-start(bf16[64,1152]{1,0:T(8,128)(2,1)S(1)} %get-tuple-element.9), channel_id=1, source_target_pairs={{0,16},{4,20},{8,24},{12,28},{16,0},{20,4},{24,8},{28,12},{1,17},{... | collective-permute-start | bytes 442376 | tf_op jit(solution)/shard_map/ppermute | solution.py:20
  48.0 6.0 %collective-permute-start.15 = (bf16[64,1152]{1,0:T(8,128)(2,1)S(1)}, bf16[64,1152]{1,0:T(8,128)(2,1)S(1)}, u32[]{:S(2)}, u32[]{:S(2)}) collective-permute-start(bf16[64,1152]{1,0:T(8,128)(2,1)S(1)} %get-tuple-element.8), channel_id=1, source_target_pairs={{0,8},{4,12},{8,0},{12,4},{16,24},{20,28},{24,16},{28,20},{1,9},{5... | collective-permute-start | bytes 442376 | tf_op jit(solution)/shard_map/ppermute | solution.py:20
  54.0 14.0 %copy-start.4 = (bf16[6,4096]{1,0:T(8,128)(2,1)S(1)}, bf16[6,4096]{1,0:T(8,128)(2,1)}, u32[]{:S(2)}) copy-start(bf16[6,4096]{1,0:T(8,128)(2,1)} %param.22) | copy-start | bytes 147460
  54.6 13.5 %copy-start.2 = (bf16[16,4096]{1,0:T(8,128)(2,1)S(1)}, bf16[16,4096]{1,0:T(8,128)(2,1)}, u32[]{:S(2)}) copy-start(bf16[16,4096]{1,0:T(8,128)(2,1)} %param.21) | copy-start | bytes 393220
  54.6 13.5 %copy-start.5 = (f32[4096]{0:T(1024)S(1)}, f32[4096]{0:T(1024)}, u32[]{:S(2)}) copy-start(f32[4096]{0:T(1024)} %param.24) | copy-start | bytes 49156
  54.6 1.3 %collective-permute-start.16 = (bf16[32,1024]{1,0:T(8,128)(2,1)S(1)}, bf16[32,1024]{1,0:T(8,128)(2,1)S(1)}, u32[]{:S(2)}, u32[]{:S(2)}) collective-permute-start(bf16[32,1024]{1,0:T(8,128)(2,1)S(1)} %slice.190), channel_id=1, source_target_pairs={{0,1},{1,0},{2,3},{3,2},{4,5},{5,4},{6,7},{7,6},{8,9},{9,8},{10,11... | collective-permute-start | bytes 196616 | tf_op jit(solution)/shard_map/ppermute | solution.py:20
  55.9 4.3 %collective-permute-start.17 = (bf16[16,2048]{1,0:T(8,128)(2,1)S(1)}, bf16[16,2048]{1,0:T(8,128)(2,1)S(1)}, u32[]{:S(2)}, u32[]{:S(2)}) collective-permute-start(bf16[16,2048]{1,0:T(8,128)(2,1)S(1)} %pad_maximum_fusion.6), channel_id=1, source_target_pairs={{0,2},{1,3},{2,0},{3,1},{4,6},{5,7},{6,4},{7,5},{8,10},{9,11},{10,... | collective-permute-start | bytes 196616 | tf_op jit(solution)/shard_map/ppermute | solution.py:20
  60.6 7.4 %collective-permute-start.18 = (bf16[6,4096]{1,0:T(8,128)(2,1)S(1)}, bf16[6,4096]{1,0:T(8,128)(2,1)S(1)}, u32[]{:S(2)}, u32[]{:S(2)}) collective-permute-start(bf16[6,4096]{1,0:T(8,128)(2,1)S(1)} %slice.193), channel_id=1, source_target_pairs={{0,1},{1,2},{2,3},{3,4},{4,5},{5,6},{6,7},{7,8},{8,9},{9,10},{10,1... | collective-permute-start | bytes 147464 | tf_op jit(solution)/shard_map/ppermute | solution.py:238

commit v2 on v1

v2 whole, which is shorter than its diff:
```python
import functools
import math

import jax
import jax.numpy as jnp
from jax import lax
from jax.experimental import pallas as pl
from jax.experimental.pallas import tpu as pltpu
from jax.sharding import PartitionSpec as P

DH = 128
MASKED = -(2.0**100)
EXP2_SCALE = math.log2(math.e) / math.sqrt(DH)
VMEM = pl.BlockSpec(memory_space=pltpu.VMEM)
SMEM = pl.BlockSpec(memory_space=pltpu.SMEM)
PARAMS = pltpu.CompilerParams(vmem_limit_bytes=40 * 2**20)


def swap(block, axis, distance):
    return lax.ppermute(
        block, axis, [(i, i ^ distance) for i in range(lax.axis_size(axis))]
    )


def after(block, *earlier):
    return lax.optimization_barrier((block, *earlier))[0]


def attend_kernel(starts, limit, newpos, q, k, v, k_new, v_new, out, *, rows_each):
    rows, slots, fresh = q.shape[0], k.shape[0], k_new.shape[0]
    heads = q.shape[1] // DH
    bias = jnp.where(
        lax.broadcasted_iota(jnp.int32, (1, slots), 1) < limit[0], 0.0, MASKED
    ).astype(jnp.float32)
    in_block = lax.broadcasted_iota(jnp.int32, (rows_each, fresh), 0)
    positions = jnp.concatenate(
        [in_block + starts[b] for b in range(rows // rows_each)], axis=0
    )
    visible = newpos[...] <= positions
    lane = lax.broadcasted_iota(jnp.int32, (rows, DH), 1)
    stats = jnp.zeros((rows, DH), jnp.float32)
    ones = jnp.ones((slots, DH), jnp.bfloat16)
    ones_new = jnp.ones((fresh, DH), jnp.bfloat16)
    across = (((1,), (1,)), ((), ()))
    def score(h):
        cols = slice(h * DH, (h + 1) * DH)
        queries = q[:, cols]
        scores = lax.dot_general(queries, k[:, cols], across, preferred_element_type=jnp.float32)
        scores_new = lax.dot_general(
            queries, k_new[:, cols], across, preferred_element_type=jnp.float32
        )
        return scores + bias, jnp.where(visible, scores_new, MASKED)

    def weigh_keys(scores, scores_new):
        top = jnp.maximum(
            jnp.max(scores, axis=1, keepdims=True), jnp.max(scores_new, axis=1, keepdims=True)
        )
        top = top.astype(jnp.bfloat16).astype(jnp.float32)
        weights = jnp.exp2((scores - top) * EXP2_SCALE).astype(jnp.bfloat16)
        weights_new = jnp.exp2((scores_new - top) * EXP2_SCALE).astype(jnp.bfloat16)
        return top, weights, weights_new

    def apply_values(h, stats, top, weights, weights_new):
        cols = slice(h * DH, (h + 1) * DH)
        both = jnp.dot(
            weights,
            jnp.concatenate([v[:, cols], ones], axis=1),
            preferred_element_type=jnp.float32,
        ) + jnp.dot(
            weights_new,
            jnp.concatenate([v_new[:, cols], ones_new], axis=1),
            preferred_element_type=jnp.float32,
        )
        out[:, cols] = both[:, :DH].astype(jnp.bfloat16)
        total = both[:, DH:]
        coarse = total.astype(jnp.bfloat16).astype(jnp.float32)
        stats = jnp.where(lane == h, top, stats)
        stats = jnp.where(lane == heads + h, coarse, stats)
        return jnp.where(lane == 2 * heads + h, total - coarse, stats)

    scored = [score(h) for h in range(heads)]
    weighed = [weigh_keys(*pair) for pair in scored]
    for h in range(heads):
        stats = apply_values(h, stats, *weighed[h])
    out[:, heads * DH :] = stats.astype(jnp.bfloat16)


def attend(starts, limit, newpos, q, k, v, k_new, v_new, rows_each):
    rows, width = q.shape
    keys = k.shape[0] + k_new.shape[0]
    return pl.pallas_call(
        functools.partial(attend_kernel, rows_each=rows_each),
        out_shape=jax.ShapeDtypeStruct((rows, width + DH), jnp.bfloat16),
        in_specs=[SMEM, SMEM] + [VMEM] * 6,
        out_specs=VMEM,
        compiler_params=PARAMS,
        cost_estimate=pl.CostEstimate(
            flops=4 * rows * keys * width,
            bytes_accessed=4 * keys * width + 4 * rows * width,
            transcendentals=rows * keys * width // DH,
        ),
        name="attend",
    )(starts, limit, newpos, q, k, v, k_new, v_new)


def prepare_kernel(place, k, v, kept, sent, *, chips):
    tokens, width = k.shape[0], kept.shape[1]
    chip, core = place[0], place[1]
    for n in range(chips):
        group = (chip ^ n) * 2
        mine = pl.ds(pl.multiple_of((group + core) * width, DH), width)
        his = pl.ds(pl.multiple_of((group + 1 - core) * width, DH), width)
        for i, ref in enumerate((k, v)):
            rows = slice((2 * n + i) * tokens, (2 * n + i + 1) * tokens)
            kept[rows, :] = ref[:, mine]
            sent[rows, :] = ref[:, his]


def prepare(place, k, v, chips, width):
    tokens = k.shape[0]
    shape = jax.ShapeDtypeStruct((chips * 2 * tokens, width), k.dtype)
    return pl.pallas_call(
        functools.partial(prepare_kernel, chips=chips),
        out_shape=[shape, shape],
        in_specs=[SMEM] + [VMEM] * 2,
        out_specs=[VMEM, VMEM],
        compiler_params=PARAMS,
        cost_estimate=pl.CostEstimate(flops=0, bytes_accessed=8 * k.size, transcendentals=0),
        name="prepare",
    )(place, k, v)


def weigh(blocks, heads):
    stats = [b[:, heads * DH :].astype(jnp.float32) for b in blocks]
    top = functools.reduce(jnp.maximum, [s[:, :heads] for s in stats])
    factors = [jnp.exp2((s[:, :heads] - top) * EXP2_SCALE) for s in stats]
    total = sum(
        f * (s[:, heads : 2 * heads] + s[:, 2 * heads : 3 * heads])
        for f, s in zip(factors, stats)
    )
    return top, factors, total


def mix(blocks, factors, h):
    cols = slice(h * DH, (h + 1) * DH)
    return sum(b[:, cols].astype(jnp.float32) * f[:, h : h + 1] for b, f in zip(blocks, factors))


def merge_kernel(*refs, sides, nears, count):
    parts, outs = refs[: sides * nears], refs[sides * nears :]
    heads = (parts[0].shape[1] - DH) // DH
    rows = parts[0].shape[0]
    for n in range(nears):
        blocks = [parts[side * nears + n] for side in range(sides)]
        top, factors, total = weigh(blocks, heads)
        coarse = total.astype(jnp.bfloat16).astype(jnp.float32)
        rest = jnp.zeros((rows, DH - 3 * heads), jnp.float32)
        stats = jnp.concatenate([top, coarse, total - coarse, rest], axis=1).astype(jnp.bfloat16)
        pieces = [mix(blocks, factors, h).astype(jnp.bfloat16) for h in range(heads)]
        for i in range(len(outs)):
            source, target = slice(i * count, (i + 1) * count), slice(n * count, (n + 1) * count)
            for h in range(heads):
                outs[i][target, h * DH : (h + 1) * DH] = pieces[h][source]
            outs[i][target, heads * DH :] = stats[source]


def merge(parts, sides, nears, count):
    rows, width = parts[0].shape
    shape = jax.ShapeDtypeStruct((nears * count, width), jnp.bfloat16)
    return pl.pallas_call(
        functools.partial(merge_kernel, sides=sides, nears=nears, count=count),
        out_shape=[shape] * (rows // count),
        in_specs=[VMEM] * len(parts),
        out_specs=[VMEM] * (rows // count),
        compiler_params=PARAMS,
        cost_estimate=pl.CostEstimate(
            flops=4 * len(parts) * rows * width,
            bytes_accessed=4 * len(parts) * rows * width,
            transcendentals=rows * 8,
        ),
        name="merge",
    )(*parts)


def finish_kernel(*refs):
    parts, out = refs[:-1], refs[-1]
    heads = out.shape[1] // DH
    _, factors, total = weigh(parts, heads)
    factors = [f / total for f in factors]
    for h in range(heads):
        out[:, h * DH : (h + 1) * DH] = mix(parts, factors, h).astype(jnp.bfloat16)


def finish(parts):
    rows, width = parts[0].shape
    return pl.pallas_call(
        finish_kernel,
        out_shape=jax.ShapeDtypeStruct((rows, width - DH), jnp.bfloat16),
        in_specs=[VMEM] * len(parts),
        out_specs=VMEM,
        compiler_params=PARAMS,
        cost_estimate=pl.CostEstimate(
            flops=4 * len(parts) * rows * width,
            bytes_accessed=2 * (len(parts) + 1) * rows * width,
            transcendentals=rows * 8,
        ),
        name="finish",
    )(*parts)


def body(
    q_new,
    k_new,
    v_new,
    cache_k,
    cache_v,
    filled_slots,
    norm_gain,
    v_branch,
    x_gate,
    conv_state,
    conv_filter,
    skip_gain,
):
    ctx_size, uly_size = lax.axis_size("ctx"), lax.axis_size("uly")
    ctx, uly = lax.axis_index("ctx"), lax.axis_index("uly")
    chip, core, chips = uly // 2, uly % 2, uly_size // 2
    tokens, channels = q_new.shape
    slots, width = cache_k.shape
    pair = 2 * tokens
    axes = ("ctx", "uly")
    count = ctx_size * uly_size
    places = [(side, near) for side in range(2) for near in range(chips)]

    def route(block, side, near):
        if side == 0 and near == 0:
            return block
        flip = side * uly_size + 2 * near
        return lax.ppermute(block, axes, [(i, i ^ flip) for i in range(count)])

    def starts_of(far, side, near):
        owner = (ctx ^ (far + side)) * uly_size + (uly ^ jnp.arange(2 * near, 2 * near + 2))
        return (owner * tokens).astype(jnp.int32)

    limit = jnp.clip(filled_slots - ctx * slots, 0, slots).astype(jnp.int32)
    newpos = jnp.concatenate([starts_of(0, 0, n) for n in range(chips)])
    newpos = (newpos[:, None] + jnp.arange(tokens, dtype=jnp.int32)[None, :]).reshape(1, -1)

    place = jnp.stack([chip, core]).astype(jnp.int32)

    def columns(block, near, half):
        return lax.dynamic_slice_in_dim(block, ((chip ^ near) * 2 + half) * width, width, 1)

    sent = jnp.concatenate([columns(q_new, n, 1 - core) for n in range(chips)], axis=0)
    received = swap(sent, "uly", 1)
    here = jnp.concatenate(
        [
            part
            for n in range(chips)
            for part in (columns(q_new, n, core), received[n * tokens : (n + 1) * tokens])
        ],
        axis=0,
    )
    blocks = {0: here}
    for far in [2, *range(ctx_size - 2, 2, -2)]:
        blocks[far] = swap(here, "ctx", far)
    chunks = [[far, far + 2] for far in range(0, ctx_size, 4)]
    kept, sent = prepare(place, k_new, v_new, chips, width)
    pairs = [b.reshape(chips, pair, width) for b in (kept, swap(sent, "uly", 1))]
    fresh_parts = [jnp.concatenate([b[n] for b in pairs], axis=0) for n in range(chips)]
    spread, fresh = [], [fresh_parts[0]]
    for i, chunk in enumerate(chunks):
        sent = [
            jnp.concatenate([blocks[far][n * pair : (n + 1) * pair] for far in chunk], axis=0)
            for n in range(chips)
        ]
        if i:
            sent = [after(block, spread[i - 1][1, 0]) for block in sent]
        got = {}
        for side, n in places:
            if i == 0 and side == 0 and n:
                whole = route(jnp.concatenate([sent[n], fresh_parts[n]], axis=0), side, n)
                got[side, n] = whole[: len(chunk) * pair]
                fresh.append(whole[len(chunk) * pair :])
            else:
                got[side, n] = route(sent[n], side, n)
        spread.append(got)
    fresh = jnp.concatenate(fresh, axis=0).reshape(uly_size, 2, tokens, width)
    fresh_k = fresh[:, 0].reshape(uly_size * tokens, width)
    fresh_v = fresh[:, 1].reshape(uly_size * tokens, width)

    def run(chunk, queries):
        rows = len(chunk) * pair
        out = attend(
            jnp.concatenate([starts_of(far, *p) for p in places for far in chunk]),
            limit,
            newpos,
            jnp.concatenate([queries[p] for p in places], axis=0),
            cache_k,
            cache_v,
            fresh_k,
            fresh_v,
            tokens,
        )
        return {p: out[i * rows : (i + 1) * rows] for i, p in enumerate(places)}

    outs = []
    for chunk, queries in zip(chunks, spread):
        if outs:
            queries = {p: after(block, outs[-1][0, 0]) for p, block in queries.items()}
        outs.append(run(chunk, queries))
    merged = {}
    for chunk, out in zip(chunks[::-1], outs[::-1]):
        got = [route(out[p], *p) for p in places]
        merged |= zip(chunk, merge(got, 2, chips, pair))
    final = [merged[0]]
    for far in sorted(merged)[:0:-1]:
        final.append(swap(merged[far], "ctx", far))
    attended = finish(final).reshape(chips, 2, tokens, width)
    sibling = swap(attended[:, 1], "uly", 1)
    both = jnp.stack([attended[:, 0], sibling])
    token_rows = jnp.concatenate(
        [
            lax.dynamic_slice(both, (half ^ core, group ^ chip, 0, 0), (1, 1, tokens, width))[0, 0]
            for group in range(chips)
            for half in range(2)
        ],
        axis=1,
    )
    values32 = token_rows.astype(jnp.float32)
    normed = (
        values32
        * lax.rsqrt(jnp.mean(values32 * values32, axis=1, keepdims=True) + 1e-06)
        * norm_gain
    )
    conv_input = lax.optimization_barrier(
        (normed * v_branch.astype(jnp.float32)).astype(jnp.bfloat16)
    )
    conv_reach = conv_filter.shape[0] - 1
    incoming = lax.ppermute(conv_input[-conv_reach:], axes, [(i, i + 1) for i in range(count - 1)])
    first_device = jnp.logical_and(ctx == 0, uly == 0)
    lower_rim = jnp.where(first_device, conv_state, incoming)
    extended = jnp.concatenate([lower_rim, conv_input], axis=0).astype(jnp.float32)
    tap_table = jnp.repeat(conv_filter, conv_input.shape[1] // conv_filter.shape[1], axis=1)
    filtered = tap_table[0] * extended[conv_reach : conv_reach + tokens]
    for lag in range(1, conv_reach + 1):
        filtered = filtered + tap_table[lag] * extended[conv_reach - lag : conv_reach - lag + tokens]
    result = x_gate.astype(jnp.float32) * (filtered + skip_gain * conv_input.astype(jnp.float32))
    return result.astype(jnp.bfloat16)


def solution(mesh):
    split = P(("ctx", "uly"), None)
    in_specs = (
        split, split, split, P("ctx", "uly"), P("ctx", "uly"), P(),
        P(), split, split, P(), P(), P(),
    )
    return jax.shard_map(body, mesh=mesh, in_specs=in_specs, out_specs=split, check_vma=False)
```

time: 69.2 us -> 65.8 us (0.951)
  waiting for transfers between devices: 26.6 us -> 22.5 us
  starting transfers between devices: 22.4 us -> 25 us
  other arithmetic: 3.32 us -> 1.71 us
  Pallas kernels: 12.1 us -> 10.5 us
  local copies, waits for them, and re-layouts: 3.48 us -> 4.52 us
    ppermute x0 -> x12, starting transfers between devices: none -> 16.3 us  [route(): return lax.ppermute(block, axes, [(i, i ^ flip) for i in range(count)])]
    ppermute x18 -> x9, starting transfers between devices: 20.5 us -> 6.68 us  [swap(): lax.ppermute(block, axis, [(i, i ^ distance) for i in range(lax.axis_size...]
    ppermute x18 -> x9, waiting for transfers between devices: 22.6 us -> 14.2 us  [swap(): lax.ppermute(block, axis, [(i, i ^ distance) for i in range(lax.axis_size...]
    ppermute x0 -> x12, waiting for transfers between devices: none -> 4.54 us  [route(): return lax.ppermute(block, axes, [(i, i ^ flip) for i in range(count)])]
    pallas_call x3 -> x2, Pallas kernels: 10.6 us -> 7.93 us  [attend(): pl.pallas_call(functools.partial(attend_kernel, rows_each=rows_each), out...]
    unnamed x21 -> x23, local copies, waits for them, and re-layouts: 0.99 us -> 2.7 us
    pallas_call x3 -> x4, Pallas kernels: 1.43 us -> 2.55 us  [the longest x2 1.46 us: merge(): pl.pallas_call(functools.partial(merge_kernel, sides=sides, nears=nears,...]
    select_n x6 -> x0, other arithmetic: 1.02 us -> none  [the longest x4 0.98 us: to_heads(): kept, sent = (jnp.where(low, left, right), jnp.where(low, right, left))]
  transfers between devices with their start and end apart: 19 -> 22, of which waited for: 11 -> 12; matrix products, arithmetic and copies ran while one was open for 7% -> 3% of each run, Pallas kernels for 17% -> 9%
where the time goes in v2:
time: 65.8 us; the launch traced here: 65.5 us
  starting transfers between devices  25 us (38%)
  waiting for transfers between devices  22.5 us (34%)
  Pallas kernels  10.5 us (16%)
  local copies, waits for them, and re-layouts  4.52 us (7%)
  other arithmetic  1.71 us (3%)
  between operations  1.26 us (2%)
    ppermute x12, starting transfers between devices, route(): return lax.ppermute(block, axes, [(i, i ^ flip) for i in range(count)])  16.3 us
    ppermute x9, waiting for transfers between devices, swap(): lax.ppermute(block, axis, [(i, i ^ distance) for i in range(lax.axis_size...  14.2 us
    pallas_call x2, Pallas kernels, attend(): pl.pallas_call(functools.partial(attend_kernel, rows_each=rows_each), out...  7.93 us
    ppermute x9, starting transfers between devices, swap(): lax.ppermute(block, axis, [(i, i ^ distance) for i in range(lax.axis_size...  6.68 us
    ppermute x12, waiting for transfers between devices, route(): return lax.ppermute(block, axes, [(i, i ^ flip) for i in range(count)])  4.54 us
    ppermute x1, waiting for transfers between devices, body(): lax.ppermute(conv_input[-conv_reach:], axes, [(i, i + 1) for i in range(c...  3.83 us
    unnamed x23, local copies, waits for them, and re-layouts  2.7 us
    ppermute x1, starting transfers between devices, body(): lax.ppermute(conv_input[-conv_reach:], axes, [(i, i + 1) for i in range(c...  2.07 us
  transfers between devices with their start and end apart: 22, of which 12 were waited for; matrix products, arithmetic and copies ran while one was open for 3% of the time, Pallas kernels for 9%

profile of v2, /device:TPU:8, one launch (start us, length us, event | category | flops | bytes accessed | tf_op | source)
XLA Modules:
  0.0 65.5 jit_solution(1835245200055900642)
XLA Ops:
  0.0 0.8 %constant_dynamic-update-slice_fusion.2 = (bf16[128,1024]{1,0:T(8,128)(2,1)S(1)}, bf16[16,1024]{1,0:T(8,128)(2,1)S(1)}, bf16[16,1024]{1,0:T(8,128)(2,1)S(1)}, bf...) fusion(bf16[16,4096]{1,0:T(8,128)(2,1)} %param.12, s32[]{:T(128)S(6)} %select_n.53, ...), kind=kLoop, calls=%fused_computation.57 | loop fusion | bytes 327696
  1.0 0.9 %copy-done.2 = bf16[16,4096]{1,0:T(8,128)(2,1)S(1)} copy-done((bf16[16,4096]{1,0:T(8,128)(2,1)S(1)}, bf16[16,4096]{1,0:T(8,128)(2,1)}, u32[]{:S(2)}) %copy-start.2) | copy-done | bytes 131096
  1.9 0.9 %copy-done.3 = bf16[16,4096]{1,0:T(8,128)(2,1)S(1)} copy-done((bf16[16,4096]{1,0:T(8,128)(2,1)S(1)}, bf16[16,4096]{1,0:T(8,128)(2,1)}, u32[]{:S(2)}) %copy-start.3) | copy-done | bytes 131096
  2.8 0.6 prepare.1
  3.4 0.6 collective-permute-start.2
  5.2 3.0 %collective-permute-start.9 = (bf16[64,1024]{1,0:T(8,128)(2,1)S(1)}, bf16[64,1024]{1,0:T(8,128)(2,1)S(1)}, u32[]{:S(2)}, u32[]{:S(2)}) collective-permute-start(bf16[64,1024]{1,0:T(8,128)(2,1)S(1)} %pad_maximum_fusion.2), channel_id=1, source_target_pairs={{0,16},{4,20},{8,24},{12,28},{16,0},{20,4},{24,8},{28,12},{1,17},{... | collective-permute-start | bytes 393224 | tf_op jit(solution)/shard_map/ppermute | solution.py:20
  8.2 0.5 collective-permute-start.10
  8.7 1.0 %collective-permute-done.1 = bf16[64,1024]{1,0:T(8,128)(2,1)S(1)} collective-permute-done((bf16[64,1024]{1,0:T(8,128)(2,1)S(1)}, bf16[64,1024]{1,0:T(8,128)(2,1)S(1)}, u32[]{:S(2)}, u32[]{:S(2)}) %collective-permute-start.1) | collective-permute-done | bytes 131104 | tf_op jit(solution)/shard_map/ppermute | solution.py:20
  9.8 1.6 %collective-permute-start.4 = (bf16[64,1024]{1,0:T(8,128)(2,1)S(1)}, bf16[64,1024]{1,0:T(8,128)(2,1)S(1)}, u32[]{:S(2)}, u32[]{:S(2)}) collective-permute-start(bf16[64,1024]{1,0:T(8,128)(2,1)S(1)} %pad_maximum_fusion.4), channel_id=1, source_target_pairs={{0,4},{1,5},{2,6},{3,7},{4,0},{5,1},{6,2},{7,3},{8,12},{9,13},{10,... | collective-permute-start | bytes 393224 | tf_op jit(solution)/shard_map/ppermute | solution.py:239
  11.4 1.6 %collective-permute-start.3 = (bf16[128,1024]{1,0:T(8,128)(2,1)S(1)}, bf16[128,1024]{1,0:T(8,128)(2,1)S(1)}, u32[]{:S(2)}, u32[]{:S(2)}) collective-permute-start(bf16[128,1024]{1,0:T(8,128)(2,1)S(1)} %get-tuple-element.58), channel_id=1, source_target_pairs={{0,2},{1,3},{2,0},{3,1},{4,6},{5,7},{6,4},{7,5},{8,10},{9,11},{10,... | collective-permute-start | bytes 786440 | tf_op jit(solution)/shard_map/ppermute | solution.py:239
  13.0 0.5 collective-permute-start.5
  13.5 4.2 %collective-permute-done.9 = bf16[64,1024]{1,0:T(8,128)(2,1)S(1)} collective-permute-done((bf16[64,1024]{1,0:T(8,128)(2,1)S(1)}, bf16[64,1024]{1,0:T(8,128)(2,1)S(1)}, u32[]{:S(2)}, u32[]{:S(2)}) %collective-permute-start.9) | collective-permute-done | bytes 131104 | tf_op jit(solution)/shard_map/ppermute | solution.py:20
  17.7 2.6 %collective-permute-done.10 = bf16[64,1024]{1,0:T(8,128)(2,1)S(1)} collective-permute-done((bf16[64,1024]{1,0:T(8,128)(2,1)S(1)}, bf16[64,1024]{1,0:T(8,128)(2,1)S(1)}, u32[]{:S(2)}, u32[]{:S(2)}) %collective-permute-start.10) | collective-permute-done | bytes 131104 | tf_op jit(solution)/shard_map/ppermute | solution.py:20
  20.3 1.6 %collective-permute-start.11 = (bf16[64,1024]{1,0:T(8,128)(2,1)S(1)}, bf16[64,1024]{1,0:T(8,128)(2,1)S(1)}, u32[]{:S(2)}, u32[]{:S(2)}) collective-permute-start(bf16[64,1024]{1,0:T(8,128)(2,1)S(1)} %get-tuple-element.22), channel_id=1, source_target_pairs={{0,2},{1,3},{2,0},{3,1},{4,6},{5,7},{6,4},{7,5},{8,10},{9,11},{10,... | collective-permute-start | bytes 393224 | tf_op jit(solution)/shard_map/ppermute | solution.py:239
  21.9 1.4 %collective-permute-start.13 = (bf16[64,1024]{1,0:T(8,128)(2,1)S(1)}, bf16[64,1024]{1,0:T(8,128)(2,1)S(1)}, u32[]{:S(2)}, u32[]{:S(2)}) collective-permute-start(bf16[64,1024]{1,0:T(8,128)(2,1)S(1)} %get-tuple-element.22), channel_id=1, source_target_pairs={{0,6},{1,7},{2,4},{3,5},{4,2},{5,3},{6,0},{7,1},{8,14},{9,15},{10,... | collective-permute-start | bytes 393224 | tf_op jit(solution)/shard_map/ppermute | solution.py:239
  23.3 0.5 collective-permute-start.12
  24.0 4.0 %attend.2 = bf16[256,1152]{1,0:T(8,128)(2,1)S(1)} custom-call(s32[16]{0:T(128)S(1)} %concatenate.53.starts, s32[1]{0:T(128)S(6)} %min.6.limit, s32[1,64]{1,0:T(1,128)S(1)} %add.208.newpos, bf16[256,1024]{1,0:T(8,128)(2,1)S(1)} %constant_dynamic-update-slice_fusion.3.q, bf16[1024,1024]{1,0:T(8,128)(2,1)S(1)} %copy-done, bf16[1024,1024]{1,0:T(8,128)(2,1)S(1)} %copy-done.1, ...), custom_call_target="tpu_custom_call" | custom-call | flops 1140850688 | bytes 5505024 | tf_op jit(solution)/shard_map/attend/pallas_call | solution.py:91
  28.0 0.9 %collective-permute-done.12 = bf16[64,1024]{1,0:T(8,128)(2,1)S(1)} collective-permute-done((bf16[64,1024]{1,0:T(8,128)(2,1)S(1)}, bf16[64,1024]{1,0:T(8,128)(2,1)S(1)}, u32[]{:S(2)}, u32[]{:S(2)}) %collective-permute-start.12) | collective-permute-done | bytes 131104 | tf_op jit(solution)/shard_map/ppermute | solution.py:239
  28.9 4.0 %attend.3 = bf16[256,1152]{1,0:T(8,128)(2,1)S(1)} custom-call(s32[16]{0:T(128)S(1)} %concatenate.62.starts, s32[1]{0:T(128)S(6)} %min.6.limit, s32[1,64]{1,0:T(1,128)S(1)} %add.208.newpos, bf16[256,1024]{1,0:T(8,128)(2,1)S(1)} %pad_maximum_fusion.q, bf16[1024,1024]{1,0:T(8,128)(2,1)S(1)} %copy-done, bf16[1024,1024]{1,0:T(8,128)(2,1)S(1)} %copy-done.1, ...), custom_call_target="tpu_custom_call" | custom-call | flops 1140850688 | bytes 5505024 | tf_op jit(solution)/shard_map/attend/pallas_call | solution.py:91
  33.0 1.6 %collective-permute-start.14 = (bf16[64,1152]{1,0:T(8,128)(2,1)S(1)}, bf16[64,1152]{1,0:T(8,128)(2,1)S(1)}, u32[]{:S(2)}, u32[]{:S(2)}) collective-permute-start(bf16[64,1152]{1,0:T(8,128)(2,1)S(1)} %get-tuple-element.35), channel_id=1, source_target_pairs={{0,2},{1,3},{2,0},{3,1},{4,6},{5,7},{6,4},{7,5},{8,10},{9,11},{10,... | collective-permute-start | bytes 442376 | tf_op jit(solution)/shard_map/ppermute | solution.py:239
  34.6 1.5 %collective-permute-start.15 = (bf16[64,1152]{1,0:T(8,128)(2,1)S(1)}, bf16[64,1152]{1,0:T(8,128)(2,1)S(1)}, u32[]{:S(2)}, u32[]{:S(2)}) collective-permute-start(bf16[64,1152]{1,0:T(8,128)(2,1)S(1)} %get-tuple-element.34), channel_id=1, source_target_pairs={{0,4},{1,5},{2,6},{3,7},{4,0},{5,1},{6,2},{7,3},{8,12},{9,13},{10,... | collective-permute-start | bytes 442376 | tf_op jit(solution)/shard_map/ppermute | solution.py:239
  36.1 0.5 collective-permute-start.16
  36.5 1.5 %collective-permute-start.6 = (bf16[64,1152]{1,0:T(8,128)(2,1)S(1)}, bf16[64,1152]{1,0:T(8,128)(2,1)S(1)}, u32[]{:S(2)}, u32[]{:S(2)}) collective-permute-start(bf16[64,1152]{1,0:T(8,128)(2,1)S(1)} %get-tuple-element.39), channel_id=1, source_target_pairs={{0,2},{1,3},{2,0},{3,1},{4,6},{5,7},{6,4},{7,5},{8,10},{9,11},{10,... | collective-permute-start | bytes 442376 | tf_op jit(solution)/shard_map/ppermute | solution.py:239
  38.1 1.5 %collective-permute-start.7 = (bf16[64,1152]{1,0:T(8,128)(2,1)S(1)}, bf16[64,1152]{1,0:T(8,128)(2,1)S(1)}, u32[]{:S(2)}, u32[]{:S(2)}) collective-permute-start(bf16[64,1152]{1,0:T(8,128)(2,1)S(1)} %get-tuple-element.38), channel_id=1, source_target_pairs={{0,4},{1,5},{2,6},{3,7},{4,0},{5,1},{6,2},{7,3},{8,12},{9,13},{10,... | collective-permute-start | bytes 442376 | tf_op jit(solution)/shard_map/ppermute | solution.py:239
  39.6 1.4 %collective-permute-done.14.refs_1_ = bf16[64,1152]{1,0:T(8,128)(2,1)S(1)} collective-permute-done((bf16[64,1152]{1,0:T(8,128)(2,1)S(1)}, bf16[64,1152]{1,0:T(8,128)(2,1)S(1)}, u32[]{:S(2)}, u32[]{:S(2)}) %collective-permute-start.14) | collective-permute-done | bytes 147488 | tf_op jit(solution)/shard_map/ppermute | solution.py:239
  41.0 2.5 %collective-permute-start.8 = (bf16[64,1152]{1,0:T(8,128)(2,1)S(1)}, bf16[64,1152]{1,0:T(8,128)(2,1)S(1)}, u32[]{:S(2)}, u32[]{:S(2)}) collective-permute-start(bf16[64,1152]{1,0:T(8,128)(2,1)S(1)} %get-tuple-element.37), channel_id=1, source_target_pairs={{0,6},{1,7},{2,4},{3,5},{4,2},{5,3},{6,0},{7,1},{8,14},{9,15},{10,... | collective-permute-start | bytes 442376 | tf_op jit(solution)/shard_map/ppermute | solution.py:239
  43.4 1.1 %collective-permute-done.16.refs_3_ = bf16[64,1152]{1,0:T(8,128)(2,1)S(1)} collective-permute-done((bf16[64,1152]{1,0:T(8,128)(2,1)S(1)}, bf16[64,1152]{1,0:T(8,128)(2,1)S(1)}, u32[]{:S(2)}, u32[]{:S(2)}) %collective-permute-start.16) | collective-permute-done | bytes 147488 | tf_op jit(solution)/shard_map/ppermute | solution.py:239
  44.5 0.7 %merge.3 = (bf16[64,1152]{1,0:T(8,128)(2,1)S(1)}, bf16[64,1152]{1,0:T(8,128)(2,1)S(1)}) custom-call(bf16[64,1152]{1,0:T(8,128)(2,1)S(1)} %get-tuple-element.36.refs_0_, bf16[64,1152]{1,0:T(8,128)(2,1)S(1)} %collective-permute-done.14.refs_1_, bf16[64,1152]{1,0:T(8,128)(2,1)S(1)} %collective-permute-done.15.refs_2_, ...), custom_call_target="tpu_custom_call" | custom-call | flops 1179648 | bytes 1179648 | tf_op jit(solution)/shard_map/merge/pallas_call | solution.py:170
  45.2 1.6 %collective-permute-start.17 = (bf16[64,1152]{1,0:T(8,128)(2,1)S(1)}, bf16[64,1152]{1,0:T(8,128)(2,1)S(1)}, u32[]{:S(2)}, u32[]{:S(2)}) collective-permute-start(bf16[64,1152]{1,0:T(8,128)(2,1)S(1)} %get-tuple-element.26), channel_id=1, source_target_pairs={{0,24},{4,28},{8,16},{12,20},{16,8},{20,12},{24,0},{28,4},{1,25},{... | collective-permute-start | bytes 442376 | tf_op jit(solution)/shard_map/ppermute | solution.py:20
  46.9 1.2 %collective-permute-done.8.refs_3_ = bf16[64,1152]{1,0:T(8,128)(2,1)S(1)} collective-permute-done((bf16[64,1152]{1,0:T(8,128)(2,1)S(1)}, bf16[64,1152]{1,0:T(8,128)(2,1)S(1)}, u32[]{:S(2)}, u32[]{:S(2)}) %collective-permute-start.8) | collective-permute-done | bytes 147488 | tf_op jit(solution)/shard_map/ppermute | solution.py:239
  48.1 0.7 %merge.2 = (bf16[64,1152]{1,0:T(8,128)(2,1)S(1)}, bf16[64,1152]{1,0:T(8,128)(2,1)S(1)}) custom-call(bf16[64,1152]{1,0:T(8,128)(2,1)S(1)} %get-tuple-element.40.refs_0_, bf16[64,1152]{1,0:T(8,128)(2,1)S(1)} %collective-permute-done.6.refs_1_, bf16[64,1152]{1,0:T(8,128)(2,1)S(1)} %collective-permute-done.7.refs_2_, ...), custom_call_target="tpu_custom_call" | custom-call | flops 1179648 | bytes 1179648 | tf_op jit(solution)/shard_map/merge/pallas_call | solution.py:170
  48.8 0.8 %collective-permute-start.19 = (bf16[64,1152]{1,0:T(8,128)(2,1)S(1)}, bf16[64,1152]{1,0:T(8,128)(2,1)S(1)}, u32[]{:S(2)}, u32[]{:S(2)}) collective-permute-start(bf16[64,1152]{1,0:T(8,128)(2,1)S(1)} %get-tuple-element.28), channel_id=1, source_target_pairs={{0,8},{4,12},{8,0},{12,4},{16,24},{20,28},{24,16},{28,20},{1,9},{5... | collective-permute-start | bytes 442376 | tf_op jit(solution)/shard_map/ppermute | solution.py:20
  49.6 1.3 %collective-permute-done.17.refs_1_ = bf16[64,1152]{1,0:T(8,128)(2,1)S(1)} collective-permute-done((bf16[64,1152]{1,0:T(8,128)(2,1)S(1)}, bf16[64,1152]{1,0:T(8,128)(2,1)S(1)}, u32[]{:S(2)}, u32[]{:S(2)}) %collective-permute-start.17) | collective-permute-done | bytes 147488 | tf_op jit(solution)/shard_map/ppermute | solution.py:20
  51.0 3.0 %collective-permute-done.18.refs_2_ = bf16[64,1152]{1,0:T(8,128)(2,1)S(1)} collective-permute-done((bf16[64,1152]{1,0:T(8,128)(2,1)S(1)}, bf16[64,1152]{1,0:T(8,128)(2,1)S(1)}, u32[]{:S(2)}, u32[]{:S(2)}) %collective-permute-start.18) | collective-permute-done | bytes 147488 | tf_op jit(solution)/shard_map/ppermute | solution.py:20
  54.0 0.9 %collective-permute-done.19.refs_3_ = bf16[64,1152]{1,0:T(8,128)(2,1)S(1)} collective-permute-done((bf16[64,1152]{1,0:T(8,128)(2,1)S(1)}, bf16[64,1152]{1,0:T(8,128)(2,1)S(1)}, u32[]{:S(2)}, u32[]{:S(2)}) %collective-permute-start.19) | collective-permute-done | bytes 147488 | tf_op jit(solution)/shard_map/ppermute | solution.py:20
  54.8 0.5 finish.1
  55.5 1.2 %collective-permute-done.20 = bf16[2,16,1024]{2,1,0:T(8,128)(2,1)S(1)} collective-permute-done((bf16[2,16,1024]{2,1,0:T(8,128)(2,1)S(1)}, bf16[2,16,1024]{2,1,0:T(8,128)(2,1)S(1)}, u32[]{:S(2)}, u32[]{:S(2)}) %collective-permute-start.20) | collective-permute-done | bytes 65568 | tf_op jit(solution)/shard_map/ppermute | solution.py:20
  56.8 0.1 fusion
  57.0 0.1 fusion.3
  57.1 2.1 %collective-permute-start.21 = (bf16[6,4096]{1,0:T(8,128)(2,1)S(1)}, bf16[6,4096]{1,0:T(8,128)(2,1)S(1)}, u32[]{:S(2)}, u32[]{:S(2)}) collective-permute-start(bf16[6,4096]{1,0:T(8,128)(2,1)S(1)} %slice.231), channel_id=1, source_target_pairs={{0,1},{1,2},{2,3},{3,4},{4,5},{5,6},{6,7},{7,8},{8,9},{9,10},{10,1... | collective-permute-start | bytes 147464 | tf_op jit(solution)/shard_map/ppermute | solution.py:340
  59.3 0.1 broadcast_in_dim.35
  59.5 0.1 broadcast_in_dim.37
  59.7 0.1 broadcast_in_dim.39
  59.9 0.1 broadcast_in_dim.41
  60.1 0.1 broadcast_in_dim.43
  60.5 0.1 broadcast_in_dim.47
  60.7 3.8 %collective-permute-done.21 = bf16[6,4096]{1,0:T(8,128)(2,1)S(1)} collective-permute-done((bf16[6,4096]{1,0:T(8,128)(2,1)S(1)}, bf16[6,4096]{1,0:T(8,128)(2,1)S(1)}, u32[]{:S(2)}, u32[]{:S(2)}) %collective-permute-start.21) | collective-permute-done | bytes 49184 | tf_op jit(solution)/shard_map/ppermute | solution.py:340
  64.6 0.9 %fusion.7 = bf16[16,4096]{1,0:T(8,128)(2,1)} fusion(f32[22,4096]{1,0:T(8,128)S(1)} %maximum_convert_fusion, bf16[16,4096]{1,0:T(8,128)(2,1)S(1)} %fusion.3, bf16[16,4096]{1,0:T(8,128)(2,1)S(1)} %copy-done.4, f32[4096]{0:T(1024)S(1)} %copy-done.7, f32[4096]{0:T(1024)S(1)} %broadcast_in_dim.47, f32[4096]{0:T(1024)S(1)} %broadcast_in_dim.45, ...), kind=kLoop, calls=%fused_computation.11 | loop fusion | flops 1245184 | bytes 2359296 | tf_op jit(solution)/shard_map/convert_element_type | solution.py:349
  (80 shorter events, 2.0 us)
Async XLA Ops:
  0.8 3.3 %collective-permute-start = (bf16[32,1024]{1,0:T(8,128)(2,1)S(1)}, bf16[32,1024]{1,0:T(8,128)(2,1)S(1)}, u32[]{:S(2)}, u32[]{:S(2)}) collective-permute-start(bf16[32,1024]{1,0:T(8,128)(2,1)S(1)} %pad_maximum_fusion.9), channel_id=1, source_target_pairs={{0,1},{1,0},{2,3},{3,2},{4,5},{5,4},{6,7},{7,6},{8,9},{9,8},{10,11... | collective-permute-start | bytes 196616 | tf_op jit(solution)/shard_map/ppermute | solution.py:20
  1.0 0.9 %copy-start.2 = (bf16[16,4096]{1,0:T(8,128)(2,1)S(1)}, bf16[16,4096]{1,0:T(8,128)(2,1)}, u32[]{:S(2)}) copy-start(bf16[16,4096]{1,0:T(8,128)(2,1)} %k.3) | copy-start | bytes 393220
  1.9 0.9 %copy-start.3 = (bf16[16,4096]{1,0:T(8,128)(2,1)S(1)}, bf16[16,4096]{1,0:T(8,128)(2,1)}, u32[]{:S(2)}) copy-start(bf16[16,4096]{1,0:T(8,128)(2,1)} %v.3) | copy-start | bytes 393220
  3.4 8.0 %collective-permute-start.2 = (bf16[64,1024]{1,0:T(8,128)(2,1)S(1)}, bf16[64,1024]{1,0:T(8,128)(2,1)S(1)}, u32[]{:S(2)}, u32[]{:S(2)}) collective-permute-start(bf16[64,1024]{1,0:T(8,128)(2,1)S(1)} %get-tuple-element.18), channel_id=1, source_target_pairs={{0,1},{1,0},{2,3},{3,2},{4,5},{5,4},{6,7},{7,6},{8,9},{9,8},{10,11... | collective-permute-start | bytes 393224 | tf_op jit(solution)/shard_map/ppermute | solution.py:20
  4.2 5.5 %collective-permute-start.1 = (bf16[64,1024]{1,0:T(8,128)(2,1)S(1)}, bf16[64,1024]{1,0:T(8,128)(2,1)S(1)}, u32[]{:S(2)}, u32[]{:S(2)}) collective-permute-start(bf16[64,1024]{1,0:T(8,128)(2,1)S(1)} %pad_maximum_fusion.2), channel_id=1, source_target_pairs={{0,8},{4,12},{8,0},{12,4},{16,24},{20,28},{24,16},{28,20},{1,9},{5... | collective-permute-start | bytes 393224 | tf_op jit(solution)/shard_map/ppermute | solution.py:20
  5.2 12.5 %collective-permute-start.9 = (bf16[64,1024]{1,0:T(8,128)(2,1)S(1)}, bf16[64,1024]{1,0:T(8,128)(2,1)S(1)}, u32[]{:S(2)}, u32[]{:S(2)}) collective-permute-start(bf16[64,1024]{1,0:T(8,128)(2,1)S(1)} %pad_maximum_fusion.2), channel_id=1, source_target_pairs={{0,16},{4,20},{8,24},{12,28},{16,0},{20,4},{24,8},{28,12},{1,17},{... | collective-permute-start | bytes 393224 | tf_op jit(solution)/shard_map/ppermute | solution.py:20
  8.2 12.0 %collective-permute-start.10 = (bf16[64,1024]{1,0:T(8,128)(2,1)S(1)}, bf16[64,1024]{1,0:T(8,128)(2,1)S(1)}, u32[]{:S(2)}, u32[]{:S(2)}) collective-permute-start(bf16[64,1024]{1,0:T(8,128)(2,1)S(1)} %pad_maximum_fusion.2), channel_id=1, source_target_pairs={{0,24},{4,28},{8,16},{12,20},{16,8},{20,12},{24,0},{28,4},{1,25},{... | collective-permute-start | bytes 393224 | tf_op jit(solution)/shard_map/ppermute | solution.py:20
  9.7 14.2 %copy-start = (bf16[1024,1024]{1,0:T(8,128)(2,1)S(1)}, bf16[1024,1024]{1,0:T(8,128)(2,1)}, u32[]{:S(2)}) copy-start(bf16[1024,1024]{1,0:T(8,128)(2,1)} %k.5) | copy-start | bytes 6291460
  9.7 14.2 %copy-start.1 = (bf16[1024,1024]{1,0:T(8,128)(2,1)S(1)}, bf16[1024,1024]{1,0:T(8,128)(2,1)}, u32[]{:S(2)}) copy-start(bf16[1024,1024]{1,0:T(8,128)(2,1)} %v.5) | copy-start | bytes 6291460
  9.8 10.5 %collective-permute-start.4 = (bf16[64,1024]{1,0:T(8,128)(2,1)S(1)}, bf16[64,1024]{1,0:T(8,128)(2,1)S(1)}, u32[]{:S(2)}, u32[]{:S(2)}) collective-permute-start(bf16[64,1024]{1,0:T(8,128)(2,1)S(1)} %pad_maximum_fusion.4), channel_id=1, source_target_pairs={{0,4},{1,5},{2,6},{3,7},{4,0},{5,1},{6,2},{7,3},{8,12},{9,13},{10,... | collective-permute-start | bytes 393224 | tf_op jit(solution)/shard_map/ppermute | solution.py:239
  11.4 12.5 %collective-permute-start.3 = (bf16[128,1024]{1,0:T(8,128)(2,1)S(1)}, bf16[128,1024]{1,0:T(8,128)(2,1)S(1)}, u32[]{:S(2)}, u32[]{:S(2)}) collective-permute-start(bf16[128,1024]{1,0:T(8,128)(2,1)S(1)} %get-tuple-element.58), channel_id=1, source_target_pairs={{0,2},{1,3},{2,0},{3,1},{4,6},{5,7},{6,4},{7,5},{8,10},{9,11},{10,... | collective-permute-start | bytes 786440 | tf_op jit(solution)/shard_map/ppermute | solution.py:239
  13.0 11.0 %collective-permute-start.5 = (bf16[64,1024]{1,0:T(8,128)(2,1)S(1)}, bf16[64,1024]{1,0:T(8,128)(2,1)S(1)}, u32[]{:S(2)}, u32[]{:S(2)}) collective-permute-start(bf16[64,1024]{1,0:T(8,128)(2,1)S(1)} %pad_maximum_fusion.5), channel_id=1, source_target_pairs={{0,6},{1,7},{2,4},{3,5},{4,2},{5,3},{6,0},{7,1},{8,14},{9,15},{10,... | collective-permute-start | bytes 393224 | tf_op jit(solution)/shard_map/ppermute | solution.py:239
  20.3 7.7 %collective-permute-start.11 = (bf16[64,1024]{1,0:T(8,128)(2,1)S(1)}, bf16[64,1024]{1,0:T(8,128)(2,1)S(1)}, u32[]{:S(2)}, u32[]{:S(2)}) collective-permute-start(bf16[64,1024]{1,0:T(8,128)(2,1)S(1)} %get-tuple-element.22), channel_id=1, source_target_pairs={{0,2},{1,3},{2,0},{3,1},{4,6},{5,7},{6,4},{7,5},{8,10},{9,11},{10,... | collective-permute-start | bytes 393224 | tf_op jit(solution)/shard_map/ppermute | solution.py:239
  21.9 7.0 %collective-permute-start.13 = (bf16[64,1024]{1,0:T(8,128)(2,1)S(1)}, bf16[64,1024]{1,0:T(8,128)(2,1)S(1)}, u32[]{:S(2)}, u32[]{:S(2)}) collective-permute-start(bf16[64,1024]{1,0:T(8,128)(2,1)S(1)} %get-tuple-element.22), channel_id=1, source_target_pairs={{0,6},{1,7},{2,4},{3,5},{4,2},{5,3},{6,0},{7,1},{8,14},{9,15},{10,... | collective-permute-start | bytes 393224 | tf_op jit(solution)/shard_map/ppermute | solution.py:239
  23.3 5.6 %collective-permute-start.12 = (bf16[64,1024]{1,0:T(8,128)(2,1)S(1)}, bf16[64,1024]{1,0:T(8,128)(2,1)S(1)}, u32[]{:S(2)}, u32[]{:S(2)}) collective-permute-start(bf16[64,1024]{1,0:T(8,128)(2,1)S(1)} %get-tuple-element.21), channel_id=1, source_target_pairs={{0,4},{1,5},{2,6},{3,7},{4,0},{5,1},{6,2},{7,3},{8,12},{9,13},{10,... | collective-permute-start | bytes 393224 | tf_op jit(solution)/shard_map/ppermute | solution.py:239
  32.9 24.1 %copy-start.5 = (bf16[16,4096]{1,0:T(8,128)(2,1)S(1)}, bf16[16,4096]{1,0:T(8,128)(2,1)}, u32[]{:S(2)}) copy-start(bf16[16,4096]{1,0:T(8,128)(2,1)} %param.19) | copy-start | bytes 393220
  32.9 24.0 %copy-start.8 = (f32[4096]{0:T(1024)S(1)}, f32[4096]{0:T(1024)}, u32[]{:S(2)}) copy-start(f32[4096]{0:T(1024)} %param.18) | copy-start | bytes 49156
  32.9 26.3 %copy-start.9 = (f32[7,256]{1,0:T(8,128)S(1)}, f32[7,256]{1,0:T(8,128)}, u32[]{:S(2)}) copy-start(f32[7,256]{1,0:T(8,128)} %param.22) | copy-start | bytes 21508
  33.0 8.0 %collective-permute-start.14 = (bf16[64,1152]{1,0:T(8,128)(2,1)S(1)}, bf16[64,1152]{1,0:T(8,128)(2,1)S(1)}, u32[]{:S(2)}, u32[]{:S(2)}) collective-permute-start(bf16[64,1152]{1,0:T(8,128)(2,1)S(1)} %get-tuple-element.35), channel_id=1, source_target_pairs={{0,2},{1,3},{2,0},{3,1},{4,6},{5,7},{6,4},{7,5},{8,10},{9,11},{10,... | collective-permute-start | bytes 442376 | tf_op jit(solution)/shard_map/ppermute | solution.py:239
  34.6 8.9 %collective-permute-start.15 = (bf16[64,1152]{1,0:T(8,128)(2,1)S(1)}, bf16[64,1152]{1,0:T(8,128)(2,1)S(1)}, u32[]{:S(2)}, u32[]{:S(2)}) collective-permute-start(bf16[64,1152]{1,0:T(8,128)(2,1)S(1)} %get-tuple-element.34), channel_id=1, source_target_pairs={{0,4},{1,5},{2,6},{3,7},{4,0},{5,1},{6,2},{7,3},{8,12},{9,13},{10,... | collective-permute-start | bytes 442376 | tf_op jit(solution)/shard_map/ppermute | solution.py:239
  36.1 8.4 %collective-permute-start.16 = (bf16[64,1152]{1,0:T(8,128)(2,1)S(1)}, bf16[64,1152]{1,0:T(8,128)(2,1)S(1)}, u32[]{:S(2)}, u32[]{:S(2)}) collective-permute-start(bf16[64,1152]{1,0:T(8,128)(2,1)S(1)} %get-tuple-element.33), channel_id=1, source_target_pairs={{0,6},{1,7},{2,4},{3,5},{4,2},{5,3},{6,0},{7,1},{8,14},{9,15},{10,... | collective-permute-start | bytes 442376 | tf_op jit(solution)/shard_map/ppermute | solution.py:239
  36.5 10.3 %collective-permute-start.6 = (bf16[64,1152]{1,0:T(8,128)(2,1)S(1)}, bf16[64,1152]{1,0:T(8,128)(2,1)S(1)}, u32[]{:S(2)}, u32[]{:S(2)}) collective-permute-start(bf16[64,1152]{1,0:T(8,128)(2,1)S(1)} %get-tuple-element.39), channel_id=1, source_target_pairs={{0,2},{1,3},{2,0},{3,1},{4,6},{5,7},{6,4},{7,5},{8,10},{9,11},{10,... | collective-permute-start | bytes 442376 | tf_op jit(solution)/shard_map/ppermute | solution.py:239
  38.1 8.8 %collective-permute-start.7 = (bf16[64,1152]{1,0:T(8,128)(2,1)S(1)}, bf16[64,1152]{1,0:T(8,128)(2,1)S(1)}, u32[]{:S(2)}, u32[]{:S(2)}) collective-permute-start(bf16[64,1152]{1,0:T(8,128)(2,1)S(1)} %get-tuple-element.38), channel_id=1, source_target_pairs={{0,4},{1,5},{2,6},{3,7},{4,0},{5,1},{6,2},{7,3},{8,12},{9,13},{10,... | collective-permute-start | bytes 442376 | tf_op jit(solution)/shard_map/ppermute | solution.py:239
  41.0 7.1 %collective-permute-start.8 = (bf16[64,1152]{1,0:T(8,128)(2,1)S(1)}, bf16[64,1152]{1,0:T(8,128)(2,1)S(1)}, u32[]{:S(2)}, u32[]{:S(2)}) collective-permute-start(bf16[64,1152]{1,0:T(8,128)(2,1)S(1)} %get-tuple-element.37), channel_id=1, source_target_pairs={{0,6},{1,7},{2,4},{3,5},{4,2},{5,3},{6,0},{7,1},{8,14},{9,15},{10,... | collective-permute-start | bytes 442376 | tf_op jit(solution)/shard_map/ppermute | solution.py:239
  45.2 5.7 %collective-permute-start.17 = (bf16[64,1152]{1,0:T(8,128)(2,1)S(1)}, bf16[64,1152]{1,0:T(8,128)(2,1)S(1)}, u32[]{:S(2)}, u32[]{:S(2)}) collective-permute-start(bf16[64,1152]{1,0:T(8,128)(2,1)S(1)} %get-tuple-element.26), channel_id=1, source_target_pairs={{0,24},{4,28},{8,16},{12,20},{16,8},{20,12},{24,0},{28,4},{1,25},{... | collective-permute-start | bytes 442376 | tf_op jit(solution)/shard_map/ppermute | solution.py:20
  46.9 7.1 %collective-permute-start.18 = (bf16[64,1152]{1,0:T(8,128)(2,1)S(1)}, bf16[64,1152]{1,0:T(8,128)(2,1)S(1)}, u32[]{:S(2)}, u32[]{:S(2)}) collective-permute-start(bf16[64,1152]{1,0:T(8,128)(2,1)S(1)} %get-tuple-element.27), channel_id=1, source_target_pairs={{0,16},{4,20},{8,24},{12,28},{16,0},{20,4},{24,8},{28,12},{1,17},{... | collective-permute-start | bytes 442376 | tf_op jit(solution)/shard_map/ppermute | solution.py:20
  48.8 15.7 %copy-start.6 = (bf16[6,4096]{1,0:T(8,128)(2,1)S(1)}, bf16[6,4096]{1,0:T(8,128)(2,1)}, u32[]{:S(2)}) copy-start(bf16[6,4096]{1,0:T(8,128)(2,1)} %param.21) | copy-start | bytes 147460
  48.8 6.0 %collective-permute-start.19 = (bf16[64,1152]{1,0:T(8,128)(2,1)S(1)}, bf16[64,1152]{1,0:T(8,128)(2,1)S(1)}, u32[]{:S(2)}, u32[]{:S(2)}) collective-permute-start(bf16[64,1152]{1,0:T(8,128)(2,1)S(1)} %get-tuple-element.28), channel_id=1, source_target_pairs={{0,8},{4,12},{8,0},{12,4},{16,24},{20,28},{24,16},{28,20},{1,9},{5... | collective-permute-start | bytes 442376 | tf_op jit(solution)/shard_map/ppermute | solution.py:20
  55.4 9.2 %copy-start.4 = (bf16[16,4096]{1,0:T(8,128)(2,1)S(1)}, bf16[16,4096]{1,0:T(8,128)(2,1)}, u32[]{:S(2)}) copy-start(bf16[16,4096]{1,0:T(8,128)(2,1)} %param.20) | copy-start | bytes 393220
  55.4 9.2 %copy-start.7 = (f32[4096]{0:T(1024)S(1)}, f32[4096]{0:T(1024)}, u32[]{:S(2)}) copy-start(f32[4096]{0:T(1024)} %param.23) | copy-start | bytes 49156
  55.4 1.3 %collective-permute-start.20 = (bf16[2,16,1024]{2,1,0:T(8,128)(2,1)S(1)}, bf16[2,16,1024]{2,1,0:T(8,128)(2,1)S(1)}, u32[]{:S(2)}, u32[]{:S(2)}) collective-permute-start(bf16[2,16,1024]{2,1,0:T(8,128)(2,1)S(1)} %get-tuple-element.49), channel_id=1, source_target_pairs={{0,1},{1,0},{2,3},{3,2},{4,5},{5,4},{6,7},{7,6},{8,9},{9,8},{10,11... | collective-permute-start | bytes 196616 | tf_op jit(solution)/shard_map/ppermute | solution.py:20
  57.1 7.4 %collective-permute-start.21 = (bf16[6,4096]{1,0:T(8,128)(2,1)S(1)}, bf16[6,4096]{1,0:T(8,128)(2,1)S(1)}, u32[]{:S(2)}, u32[]{:S(2)}) collective-permute-start(bf16[6,4096]{1,0:T(8,128)(2,1)S(1)} %slice.231), channel_id=1, source_target_pairs={{0,1},{1,2},{2,3},{3,4},{4,5},{5,6},{6,7},{7,8},{8,9},{9,10},{10,1... | collective-permute-start | bytes 147464 | tf_op jit(solution)/shard_map/ppermute | solution.py:340

commit v3 on v2

--- a/solution.py
+++ b/solution.py
@@ -150,18 +150,20 @@
     parts, outs = refs[: sides * nears], refs[sides * nears :]
     heads = (parts[0].shape[1] - DH) // DH
     rows = parts[0].shape[0]
-    for n in range(nears):
-        blocks = [parts[side * nears + n] for side in range(sides)]
-        top, factors, total = weigh(blocks, heads)
-        coarse = total.astype(jnp.bfloat16).astype(jnp.float32)
-        rest = jnp.zeros((rows, DH - 3 * heads), jnp.float32)
-        stats = jnp.concatenate([top, coarse, total - coarse, rest], axis=1).astype(jnp.bfloat16)
-        pieces = [mix(blocks, factors, h).astype(jnp.bfloat16) for h in range(heads)]
-        for i in range(len(outs)):
-            source, target = slice(i * count, (i + 1) * count), slice(n * count, (n + 1) * count)
-            for h in range(heads):
-                outs[i][target, h * DH : (h + 1) * DH] = pieces[h][source]
-            outs[i][target, heads * DH :] = stats[source]
+    blocks = [
+        jnp.concatenate([parts[side * nears + n][...] for n in range(nears)], axis=0)
+        for side in range(sides)
+    ]
+    top, factors, total = weigh(blocks, heads)
+    coarse = total.astype(jnp.bfloat16).astype(jnp.float32)
+    rest = jnp.zeros((nears * rows, DH - 3 * heads), jnp.float32)
+    stats = jnp.concatenate([top, coarse, total - coarse, rest], axis=1).astype(jnp.bfloat16)
+    for h in range(heads + 1):
+        piece = mix(blocks, factors, h).astype(jnp.bfloat16) if h < heads else stats
+        for i, out in enumerate(outs):
+            for n in range(nears):
+                first = n * rows + i * count
+                out[n * count : (n + 1) * count, h * DH : (h + 1) * DH] = piece[first : first + count]
 
 
 def merge(parts, sides, nears, count):
@@ -262,7 +264,7 @@
         axis=0,
     )
     blocks = {0: here}
-    for far in [2, *range(ctx_size - 2, 2, -2)]:
+    for far in range(2, ctx_size, 2):
         blocks[far] = swap(here, "ctx", far)
     chunks = [[far, far + 2] for far in range(0, ctx_size, 4)]
     kept, sent = prepare(place, k_new, v_new, chips, width)

time: 65.8 us -> 65.5 us (level)
  transfers between devices with their start and end apart: 22 -> 22, of which waited for: 12 -> 12; matrix products, arithmetic and copies ran while one was open for 3% -> 3% of each run, Pallas kernels for 9% -> 8%
where the time goes in v3:
time: 65.5 us; the launch traced here: 65.2 us
  starting transfers between devices  24.7 us (38%)
  waiting for transfers between devices  23.1 us (35%)
  Pallas kernels  9.92 us (15%)
  local copies, waits for them, and re-layouts  4.52 us (7%)
  other arithmetic  1.71 us (3%)
  between operations  1.26 us (2%)
    ppermute x12, starting transfers between devices, route(): return lax.ppermute(block, axes, [(i, i ^ flip) for i in range(count)])  16.3 us
    ppermute x9, waiting for transfers between devices, swap(): lax.ppermute(block, axis, [(i, i ^ distance) for i in range(lax.axis_size...  14.4 us
    pallas_call x2, Pallas kernels, attend(): pl.pallas_call(functools.partial(attend_kernel, rows_each=rows_each), out...  7.93 us
    ppermute x9, starting transfers between devices, swap(): lax.ppermute(block, axis, [(i, i ^ distance) for i in range(lax.axis_size...  6.41 us
    ppermute x12, waiting for transfers between devices, route(): return lax.ppermute(block, axes, [(i, i ^ flip) for i in range(count)])  4.81 us
    ppermute x1, waiting for transfers between devices, body(): lax.ppermute(conv_input[-conv_reach:], axes, [(i, i + 1) for i in range(c...  3.83 us
    unnamed x23, local copies, waits for them, and re-layouts  2.7 us
    ppermute x1, starting transfers between devices, body(): lax.ppermute(conv_input[-conv_reach:], axes, [(i, i + 1) for i in range(c...  2.07 us
  transfers between devices with their start and end apart: 22, of which 12 were waited for; matrix products, arithmetic and copies ran while one was open for 3% of the time, Pallas kernels for 8%

profile of v3, /device:TPU:8, one launch (start us, length us, event | category | flops | bytes accessed | tf_op | source)
XLA Modules:
  0.0 65.2 jit_solution(2846817859276931108)
XLA Ops:
  0.0 0.8 %constant_dynamic-update-slice_fusion.2 = (bf16[128,1024]{1,0:T(8,128)(2,1)S(1)}, bf16[16,1024]{1,0:T(8,128)(2,1)S(1)}, bf16[16,1024]{1,0:T(8,128)(2,1)S(1)}, bf...) fusion(bf16[16,4096]{1,0:T(8,128)(2,1)} %param.12, s32[]{:T(128)S(6)} %select_n.53, ...), kind=kLoop, calls=%fused_computation.57 | loop fusion | bytes 327696
  1.0 0.9 %copy-done.2 = bf16[16,4096]{1,0:T(8,128)(2,1)S(1)} copy-done((bf16[16,4096]{1,0:T(8,128)(2,1)S(1)}, bf16[16,4096]{1,0:T(8,128)(2,1)}, u32[]{:S(2)}) %copy-start.2) | copy-done | bytes 131096
  1.9 0.9 %copy-done.3 = bf16[16,4096]{1,0:T(8,128)(2,1)S(1)} copy-done((bf16[16,4096]{1,0:T(8,128)(2,1)S(1)}, bf16[16,4096]{1,0:T(8,128)(2,1)}, u32[]{:S(2)}) %copy-start.3) | copy-done | bytes 131096
  2.8 0.6 prepare.1
  3.4 0.6 collective-permute-start.2
  5.2 3.0 %collective-permute-start.9 = (bf16[64,1024]{1,0:T(8,128)(2,1)S(1)}, bf16[64,1024]{1,0:T(8,128)(2,1)S(1)}, u32[]{:S(2)}, u32[]{:S(2)}) collective-permute-start(bf16[64,1024]{1,0:T(8,128)(2,1)S(1)} %pad_maximum_fusion.2), channel_id=1, source_target_pairs={{0,16},{4,20},{8,24},{12,28},{16,0},{20,4},{24,8},{28,12},{1,17},{... | collective-permute-start | bytes 393224 | tf_op jit(solution)/shard_map/ppermute | solution.py:20
  8.2 0.5 collective-permute-start.10
  8.7 1.0 %collective-permute-done.1 = bf16[64,1024]{1,0:T(8,128)(2,1)S(1)} collective-permute-done((bf16[64,1024]{1,0:T(8,128)(2,1)S(1)}, bf16[64,1024]{1,0:T(8,128)(2,1)S(1)}, u32[]{:S(2)}, u32[]{:S(2)}) %collective-permute-start.1) | collective-permute-done | bytes 131104 | tf_op jit(solution)/shard_map/ppermute | solution.py:20
  9.8 1.6 %collective-permute-start.4 = (bf16[64,1024]{1,0:T(8,128)(2,1)S(1)}, bf16[64,1024]{1,0:T(8,128)(2,1)S(1)}, u32[]{:S(2)}, u32[]{:S(2)}) collective-permute-start(bf16[64,1024]{1,0:T(8,128)(2,1)S(1)} %pad_maximum_fusion.4), channel_id=1, source_target_pairs={{0,4},{1,5},{2,6},{3,7},{4,0},{5,1},{6,2},{7,3},{8,12},{9,13},{10,... | collective-permute-start | bytes 393224 | tf_op jit(solution)/shard_map/ppermute | solution.py:241
  11.4 1.6 %collective-permute-start.3 = (bf16[128,1024]{1,0:T(8,128)(2,1)S(1)}, bf16[128,1024]{1,0:T(8,128)(2,1)S(1)}, u32[]{:S(2)}, u32[]{:S(2)}) collective-permute-start(bf16[128,1024]{1,0:T(8,128)(2,1)S(1)} %get-tuple-element.58), channel_id=1, source_target_pairs={{0,2},{1,3},{2,0},{3,1},{4,6},{5,7},{6,4},{7,5},{8,10},{9,11},{10,... | collective-permute-start | bytes 786440 | tf_op jit(solution)/shard_map/ppermute | solution.py:241
  13.0 0.5 collective-permute-start.5
  13.5 4.2 %collective-permute-done.9 = bf16[64,1024]{1,0:T(8,128)(2,1)S(1)} collective-permute-done((bf16[64,1024]{1,0:T(8,128)(2,1)S(1)}, bf16[64,1024]{1,0:T(8,128)(2,1)S(1)}, u32[]{:S(2)}, u32[]{:S(2)}) %collective-permute-start.9) | collective-permute-done | bytes 131104 | tf_op jit(solution)/shard_map/ppermute | solution.py:20
  17.7 2.6 %collective-permute-done.10 = bf16[64,1024]{1,0:T(8,128)(2,1)S(1)} collective-permute-done((bf16[64,1024]{1,0:T(8,128)(2,1)S(1)}, bf16[64,1024]{1,0:T(8,128)(2,1)S(1)}, u32[]{:S(2)}, u32[]{:S(2)}) %collective-permute-start.10) | collective-permute-done | bytes 131104 | tf_op jit(solution)/shard_map/ppermute | solution.py:20
  20.3 1.6 %collective-permute-start.11 = (bf16[64,1024]{1,0:T(8,128)(2,1)S(1)}, bf16[64,1024]{1,0:T(8,128)(2,1)S(1)}, u32[]{:S(2)}, u32[]{:S(2)}) collective-permute-start(bf16[64,1024]{1,0:T(8,128)(2,1)S(1)} %get-tuple-element.22), channel_id=1, source_target_pairs={{0,2},{1,3},{2,0},{3,1},{4,6},{5,7},{6,4},{7,5},{8,10},{9,11},{10,... | collective-permute-start | bytes 393224 | tf_op jit(solution)/shard_map/ppermute | solution.py:241
  21.9 1.4 %collective-permute-start.13 = (bf16[64,1024]{1,0:T(8,128)(2,1)S(1)}, bf16[64,1024]{1,0:T(8,128)(2,1)S(1)}, u32[]{:S(2)}, u32[]{:S(2)}) collective-permute-start(bf16[64,1024]{1,0:T(8,128)(2,1)S(1)} %get-tuple-element.22), channel_id=1, source_target_pairs={{0,6},{1,7},{2,4},{3,5},{4,2},{5,3},{6,0},{7,1},{8,14},{9,15},{10,... | collective-permute-start | bytes 393224 | tf_op jit(solution)/shard_map/ppermute | solution.py:241
  23.3 0.5 collective-permute-start.12
  24.0 4.0 %attend.2 = bf16[256,1152]{1,0:T(8,128)(2,1)S(1)} custom-call(s32[16]{0:T(128)S(1)} %concatenate.53.starts, s32[1]{0:T(128)S(6)} %min.6.limit, s32[1,64]{1,0:T(1,128)S(1)} %add.208.newpos, bf16[256,1024]{1,0:T(8,128)(2,1)S(1)} %constant_dynamic-update-slice_fusion.3.q, bf16[1024,1024]{1,0:T(8,128)(2,1)S(1)} %copy-done, bf16[1024,1024]{1,0:T(8,128)(2,1)S(1)} %copy-done.1, ...), custom_call_target="tpu_custom_call" | custom-call | flops 1140850688 | bytes 5505024 | tf_op jit(solution)/shard_map/attend/pallas_call | solution.py:91
  28.0 0.9 %collective-permute-done.12 = bf16[64,1024]{1,0:T(8,128)(2,1)S(1)} collective-permute-done((bf16[64,1024]{1,0:T(8,128)(2,1)S(1)}, bf16[64,1024]{1,0:T(8,128)(2,1)S(1)}, u32[]{:S(2)}, u32[]{:S(2)}) %collective-permute-start.12) | collective-permute-done | bytes 131104 | tf_op jit(solution)/shard_map/ppermute | solution.py:241
  28.9 4.0 %attend.3 = bf16[256,1152]{1,0:T(8,128)(2,1)S(1)} custom-call(s32[16]{0:T(128)S(1)} %concatenate.62.starts, s32[1]{0:T(128)S(6)} %min.6.limit, s32[1,64]{1,0:T(1,128)S(1)} %add.208.newpos, bf16[256,1024]{1,0:T(8,128)(2,1)S(1)} %pad_maximum_fusion.q, bf16[1024,1024]{1,0:T(8,128)(2,1)S(1)} %copy-done, bf16[1024,1024]{1,0:T(8,128)(2,1)S(1)} %copy-done.1, ...), custom_call_target="tpu_custom_call" | custom-call | flops 1140850688 | bytes 5505024 | tf_op jit(solution)/shard_map/attend/pallas_call | solution.py:91
  33.0 1.6 %collective-permute-start.14 = (bf16[64,1152]{1,0:T(8,128)(2,1)S(1)}, bf16[64,1152]{1,0:T(8,128)(2,1)S(1)}, u32[]{:S(2)}, u32[]{:S(2)}) collective-permute-start(bf16[64,1152]{1,0:T(8,128)(2,1)S(1)} %get-tuple-element.35), channel_id=1, source_target_pairs={{0,2},{1,3},{2,0},{3,1},{4,6},{5,7},{6,4},{7,5},{8,10},{9,11},{10,... | collective-permute-start | bytes 442376 | tf_op jit(solution)/shard_map/ppermute | solution.py:241
  34.6 1.5 %collective-permute-start.15 = (bf16[64,1152]{1,0:T(8,128)(2,1)S(1)}, bf16[64,1152]{1,0:T(8,128)(2,1)S(1)}, u32[]{:S(2)}, u32[]{:S(2)}) collective-permute-start(bf16[64,1152]{1,0:T(8,128)(2,1)S(1)} %get-tuple-element.34), channel_id=1, source_target_pairs={{0,4},{1,5},{2,6},{3,7},{4,0},{5,1},{6,2},{7,3},{8,12},{9,13},{10,... | collective-permute-start | bytes 442376 | tf_op jit(solution)/shard_map/ppermute | solution.py:241
  36.1 0.5 collective-permute-start.16
  36.5 1.5 %collective-permute-start.6 = (bf16[64,1152]{1,0:T(8,128)(2,1)S(1)}, bf16[64,1152]{1,0:T(8,128)(2,1)S(1)}, u32[]{:S(2)}, u32[]{:S(2)}) collective-permute-start(bf16[64,1152]{1,0:T(8,128)(2,1)S(1)} %get-tuple-element.39), channel_id=1, source_target_pairs={{0,2},{1,3},{2,0},{3,1},{4,6},{5,7},{6,4},{7,5},{8,10},{9,11},{10,... | collective-permute-start | bytes 442376 | tf_op jit(solution)/shard_map/ppermute | solution.py:241
  38.1 1.5 %collective-permute-start.7 = (bf16[64,1152]{1,0:T(8,128)(2,1)S(1)}, bf16[64,1152]{1,0:T(8,128)(2,1)S(1)}, u32[]{:S(2)}, u32[]{:S(2)}) collective-permute-start(bf16[64,1152]{1,0:T(8,128)(2,1)S(1)} %get-tuple-element.38), channel_id=1, source_target_pairs={{0,4},{1,5},{2,6},{3,7},{4,0},{5,1},{6,2},{7,3},{8,12},{9,13},{10,... | collective-permute-start | bytes 442376 | tf_op jit(solution)/shard_map/ppermute | solution.py:241
  39.6 1.4 %collective-permute-done.14.refs_1_ = bf16[64,1152]{1,0:T(8,128)(2,1)S(1)} collective-permute-done((bf16[64,1152]{1,0:T(8,128)(2,1)S(1)}, bf16[64,1152]{1,0:T(8,128)(2,1)S(1)}, u32[]{:S(2)}, u32[]{:S(2)}) %collective-permute-start.14) | collective-permute-done | bytes 147488 | tf_op jit(solution)/shard_map/ppermute | solution.py:241
  41.0 2.5 %collective-permute-start.8 = (bf16[64,1152]{1,0:T(8,128)(2,1)S(1)}, bf16[64,1152]{1,0:T(8,128)(2,1)S(1)}, u32[]{:S(2)}, u32[]{:S(2)}) collective-permute-start(bf16[64,1152]{1,0:T(8,128)(2,1)S(1)} %get-tuple-element.37), channel_id=1, source_target_pairs={{0,6},{1,7},{2,4},{3,5},{4,2},{5,3},{6,0},{7,1},{8,14},{9,15},{10,... | collective-permute-start | bytes 442376 | tf_op jit(solution)/shard_map/ppermute | solution.py:241
  43.4 1.1 %collective-permute-done.16.refs_3_ = bf16[64,1152]{1,0:T(8,128)(2,1)S(1)} collective-permute-done((bf16[64,1152]{1,0:T(8,128)(2,1)S(1)}, bf16[64,1152]{1,0:T(8,128)(2,1)S(1)}, u32[]{:S(2)}, u32[]{:S(2)}) %collective-permute-start.16) | collective-permute-done | bytes 147488 | tf_op jit(solution)/shard_map/ppermute | solution.py:241
  44.5 0.5 merge.3
  45.0 1.6 %collective-permute-start.17 = (bf16[64,1152]{1,0:T(8,128)(2,1)S(1)}, bf16[64,1152]{1,0:T(8,128)(2,1)S(1)}, u32[]{:S(2)}, u32[]{:S(2)}) collective-permute-start(bf16[64,1152]{1,0:T(8,128)(2,1)S(1)} %get-tuple-element.26), channel_id=1, source_target_pairs={{0,24},{4,28},{8,16},{12,20},{16,8},{20,12},{24,0},{28,4},{1,25},{... | collective-permute-start | bytes 442376 | tf_op jit(solution)/shard_map/ppermute | solution.py:20
  46.6 1.5 %collective-permute-done.8.refs_3_ = bf16[64,1152]{1,0:T(8,128)(2,1)S(1)} collective-permute-done((bf16[64,1152]{1,0:T(8,128)(2,1)S(1)}, bf16[64,1152]{1,0:T(8,128)(2,1)S(1)}, u32[]{:S(2)}, u32[]{:S(2)}) %collective-permute-start.8) | collective-permute-done | bytes 147488 | tf_op jit(solution)/shard_map/ppermute | solution.py:241
  48.1 0.5 merge.2
  48.5 0.5 collective-permute-start.19
  49.1 1.6 %collective-permute-done.17.refs_1_ = bf16[64,1152]{1,0:T(8,128)(2,1)S(1)} collective-permute-done((bf16[64,1152]{1,0:T(8,128)(2,1)S(1)}, bf16[64,1152]{1,0:T(8,128)(2,1)S(1)}, u32[]{:S(2)}, u32[]{:S(2)}) %collective-permute-start.17) | collective-permute-done | bytes 147488 | tf_op jit(solution)/shard_map/ppermute | solution.py:20
  50.7 3.0 %collective-permute-done.18.refs_2_ = bf16[64,1152]{1,0:T(8,128)(2,1)S(1)} collective-permute-done((bf16[64,1152]{1,0:T(8,128)(2,1)S(1)}, bf16[64,1152]{1,0:T(8,128)(2,1)S(1)}, u32[]{:S(2)}, u32[]{:S(2)}) %collective-permute-start.18) | collective-permute-done | bytes 147488 | tf_op jit(solution)/shard_map/ppermute | solution.py:20
  53.7 0.9 %collective-permute-done.19.refs_3_ = bf16[64,1152]{1,0:T(8,128)(2,1)S(1)} collective-permute-done((bf16[64,1152]{1,0:T(8,128)(2,1)S(1)}, bf16[64,1152]{1,0:T(8,128)(2,1)S(1)}, u32[]{:S(2)}, u32[]{:S(2)}) %collective-permute-start.19) | collective-permute-done | bytes 147488 | tf_op jit(solution)/shard_map/ppermute | solution.py:20
  54.6 0.5 finish.1
  55.2 1.2 %collective-permute-done.20 = bf16[2,16,1024]{2,1,0:T(8,128)(2,1)S(1)} collective-permute-done((bf16[2,16,1024]{2,1,0:T(8,128)(2,1)S(1)}, bf16[2,16,1024]{2,1,0:T(8,128)(2,1)S(1)}, u32[]{:S(2)}, u32[]{:S(2)}) %collective-permute-start.20) | collective-permute-done | bytes 65568 | tf_op jit(solution)/shard_map/ppermute | solution.py:20
  56.5 0.1 fusion
  56.7 0.1 fusion.3
  56.8 2.1 %collective-permute-start.21 = (bf16[6,4096]{1,0:T(8,128)(2,1)S(1)}, bf16[6,4096]{1,0:T(8,128)(2,1)S(1)}, u32[]{:S(2)}, u32[]{:S(2)}) collective-permute-start(bf16[6,4096]{1,0:T(8,128)(2,1)S(1)} %slice.231), channel_id=1, source_target_pairs={{0,1},{1,2},{2,3},{3,4},{4,5},{5,6},{6,7},{7,8},{8,9},{9,10},{10,1... | collective-permute-start | bytes 147464 | tf_op jit(solution)/shard_map/ppermute | solution.py:342
  59.0 0.1 broadcast_in_dim.35
  59.2 0.1 broadcast_in_dim.37
  59.5 0.1 broadcast_in_dim.39
  59.7 0.1 broadcast_in_dim.41
  59.9 0.1 broadcast_in_dim.43
  60.1 0.1 broadcast_in_dim.45
  60.4 3.8 %collective-permute-done.21 = bf16[6,4096]{1,0:T(8,128)(2,1)S(1)} collective-permute-done((bf16[6,4096]{1,0:T(8,128)(2,1)S(1)}, bf16[6,4096]{1,0:T(8,128)(2,1)S(1)}, u32[]{:S(2)}, u32[]{:S(2)}) %collective-permute-start.21) | collective-permute-done | bytes 49184 | tf_op jit(solution)/shard_map/ppermute | solution.py:342
  64.3 0.9 %fusion.7 = bf16[16,4096]{1,0:T(8,128)(2,1)} fusion(f32[22,4096]{1,0:T(8,128)S(1)} %maximum_convert_fusion, bf16[16,4096]{1,0:T(8,128)(2,1)S(1)} %fusion.3, bf16[16,4096]{1,0:T(8,128)(2,1)S(1)} %copy-done.4, f32[4096]{0:T(1024)S(1)} %copy-done.7, f32[4096]{0:T(1024)S(1)} %broadcast_in_dim.47, f32[4096]{0:T(1024)S(1)} %broadcast_in_dim.45, ...), kind=kLoop, calls=%fused_computation.11 | loop fusion | flops 1245184 | bytes 2359296 | tf_op jit(solution)/shard_map/convert_element_type | solution.py:351
  (80 shorter events, 2.0 us)
Async XLA Ops:
  0.8 3.3 %collective-permute-start = (bf16[32,1024]{1,0:T(8,128)(2,1)S(1)}, bf16[32,1024]{1,0:T(8,128)(2,1)S(1)}, u32[]{:S(2)}, u32[]{:S(2)}) collective-permute-start(bf16[32,1024]{1,0:T(8,128)(2,1)S(1)} %pad_maximum_fusion.9), channel_id=1, source_target_pairs={{0,1},{1,0},{2,3},{3,2},{4,5},{5,4},{6,7},{7,6},{8,9},{9,8},{10,11... | collective-permute-start | bytes 196616 | tf_op jit(solution)/shard_map/ppermute | solution.py:20
  1.0 0.9 %copy-start.2 = (bf16[16,4096]{1,0:T(8,128)(2,1)S(1)}, bf16[16,4096]{1,0:T(8,128)(2,1)}, u32[]{:S(2)}) copy-start(bf16[16,4096]{1,0:T(8,128)(2,1)} %k.3) | copy-start | bytes 393220
  1.9 0.9 %copy-start.3 = (bf16[16,4096]{1,0:T(8,128)(2,1)S(1)}, bf16[16,4096]{1,0:T(8,128)(2,1)}, u32[]{:S(2)}) copy-start(bf16[16,4096]{1,0:T(8,128)(2,1)} %v.3) | copy-start | bytes 393220
  3.4 8.0 %collective-permute-start.2 = (bf16[64,1024]{1,0:T(8,128)(2,1)S(1)}, bf16[64,1024]{1,0:T(8,128)(2,1)S(1)}, u32[]{:S(2)}, u32[]{:S(2)}) collective-permute-start(bf16[64,1024]{1,0:T(8,128)(2,1)S(1)} %get-tuple-element.18), channel_id=1, source_target_pairs={{0,1},{1,0},{2,3},{3,2},{4,5},{5,4},{6,7},{7,6},{8,9},{9,8},{10,11... | collective-permute-start | bytes 393224 | tf_op jit(solution)/shard_map/ppermute | solution.py:20
  4.2 5.5 %collective-permute-start.1 = (bf16[64,1024]{1,0:T(8,128)(2,1)S(1)}, bf16[64,1024]{1,0:T(8,128)(2,1)S(1)}, u32[]{:S(2)}, u32[]{:S(2)}) collective-permute-start(bf16[64,1024]{1,0:T(8,128)(2,1)S(1)} %pad_maximum_fusion.2), channel_id=1, source_target_pairs={{0,8},{4,12},{8,0},{12,4},{16,24},{20,28},{24,16},{28,20},{1,9},{5... | collective-permute-start | bytes 393224 | tf_op jit(solution)/shard_map/ppermute | solution.py:20
  5.2 12.5 %collective-permute-start.9 = (bf16[64,1024]{1,0:T(8,128)(2,1)S(1)}, bf16[64,1024]{1,0:T(8,128)(2,1)S(1)}, u32[]{:S(2)}, u32[]{:S(2)}) collective-permute-start(bf16[64,1024]{1,0:T(8,128)(2,1)S(1)} %pad_maximum_fusion.2), channel_id=1, source_target_pairs={{0,16},{4,20},{8,24},{12,28},{16,0},{20,4},{24,8},{28,12},{1,17},{... | collective-permute-start | bytes 393224 | tf_op jit(solution)/shard_map/ppermute | solution.py:20
  8.2 12.0 %collective-permute-start.10 = (bf16[64,1024]{1,0:T(8,128)(2,1)S(1)}, bf16[64,1024]{1,0:T(8,128)(2,1)S(1)}, u32[]{:S(2)}, u32[]{:S(2)}) collective-permute-start(bf16[64,1024]{1,0:T(8,128)(2,1)S(1)} %pad_maximum_fusion.2), channel_id=1, source_target_pairs={{0,24},{4,28},{8,16},{12,20},{16,8},{20,12},{24,0},{28,4},{1,25},{... | collective-permute-start | bytes 393224 | tf_op jit(solution)/shard_map/ppermute | solution.py:20
  9.7 14.2 %copy-start = (bf16[1024,1024]{1,0:T(8,128)(2,1)S(1)}, bf16[1024,1024]{1,0:T(8,128)(2,1)}, u32[]{:S(2)}) copy-start(bf16[1024,1024]{1,0:T(8,128)(2,1)} %k.5) | copy-start | bytes 6291460
  9.7 14.2 %copy-start.1 = (bf16[1024,1024]{1,0:T(8,128)(2,1)S(1)}, bf16[1024,1024]{1,0:T(8,128)(2,1)}, u32[]{:S(2)}) copy-start(bf16[1024,1024]{1,0:T(8,128)(2,1)} %v.5) | copy-start | bytes 6291460
  9.8 10.5 %collective-permute-start.4 = (bf16[64,1024]{1,0:T(8,128)(2,1)S(1)}, bf16[64,1024]{1,0:T(8,128)(2,1)S(1)}, u32[]{:S(2)}, u32[]{:S(2)}) collective-permute-start(bf16[64,1024]{1,0:T(8,128)(2,1)S(1)} %pad_maximum_fusion.4), channel_id=1, source_target_pairs={{0,4},{1,5},{2,6},{3,7},{4,0},{5,1},{6,2},{7,3},{8,12},{9,13},{10,... | collective-permute-start | bytes 393224 | tf_op jit(solution)/shard_map/ppermute | solution.py:241
  11.4 12.5 %collective-permute-start.3 = (bf16[128,1024]{1,0:T(8,128)(2,1)S(1)}, bf16[128,1024]{1,0:T(8,128)(2,1)S(1)}, u32[]{:S(2)}, u32[]{:S(2)}) collective-permute-start(bf16[128,1024]{1,0:T(8,128)(2,1)S(1)} %get-tuple-element.58), channel_id=1, source_target_pairs={{0,2},{1,3},{2,0},{3,1},{4,6},{5,7},{6,4},{7,5},{8,10},{9,11},{10,... | collective-permute-start | bytes 786440 | tf_op jit(solution)/shard_map/ppermute | solution.py:241
  13.0 11.0 %collective-permute-start.5 = (bf16[64,1024]{1,0:T(8,128)(2,1)S(1)}, bf16[64,1024]{1,0:T(8,128)(2,1)S(1)}, u32[]{:S(2)}, u32[]{:S(2)}) collective-permute-start(bf16[64,1024]{1,0:T(8,128)(2,1)S(1)} %pad_maximum_fusion.5), channel_id=1, source_target_pairs={{0,6},{1,7},{2,4},{3,5},{4,2},{5,3},{6,0},{7,1},{8,14},{9,15},{10,... | collective-permute-start | bytes 393224 | tf_op jit(solution)/shard_map/ppermute | solution.py:241
  20.3 7.7 %collective-permute-start.11 = (bf16[64,1024]{1,0:T(8,128)(2,1)S(1)}, bf16[64,1024]{1,0:T(8,128)(2,1)S(1)}, u32[]{:S(2)}, u32[]{:S(2)}) collective-permute-start(bf16[64,1024]{1,0:T(8,128)(2,1)S(1)} %get-tuple-element.22), channel_id=1, source_target_pairs={{0,2},{1,3},{2,0},{3,1},{4,6},{5,7},{6,4},{7,5},{8,10},{9,11},{10,... | collective-permute-start | bytes 393224 | tf_op jit(solution)/shard_map/ppermute | solution.py:241
  21.9 7.0 %collective-permute-start.13 = (bf16[64,1024]{1,0:T(8,128)(2,1)S(1)}, bf16[64,1024]{1,0:T(8,128)(2,1)S(1)}, u32[]{:S(2)}, u32[]{:S(2)}) collective-permute-start(bf16[64,1024]{1,0:T(8,128)(2,1)S(1)} %get-tuple-element.22), channel_id=1, source_target_pairs={{0,6},{1,7},{2,4},{3,5},{4,2},{5,3},{6,0},{7,1},{8,14},{9,15},{10,... | collective-permute-start | bytes 393224 | tf_op jit(solution)/shard_map/ppermute | solution.py:241
  23.3 5.6 %collective-permute-start.12 = (bf16[64,1024]{1,0:T(8,128)(2,1)S(1)}, bf16[64,1024]{1,0:T(8,128)(2,1)S(1)}, u32[]{:S(2)}, u32[]{:S(2)}) collective-permute-start(bf16[64,1024]{1,0:T(8,128)(2,1)S(1)} %get-tuple-element.21), channel_id=1, source_target_pairs={{0,4},{1,5},{2,6},{3,7},{4,0},{5,1},{6,2},{7,3},{8,12},{9,13},{10,... | collective-permute-start | bytes 393224 | tf_op jit(solution)/shard_map/ppermute | solution.py:241
  32.9 23.8 %copy-start.5 = (bf16[16,4096]{1,0:T(8,128)(2,1)S(1)}, bf16[16,4096]{1,0:T(8,128)(2,1)}, u32[]{:S(2)}) copy-start(bf16[16,4096]{1,0:T(8,128)(2,1)} %param.19) | copy-start | bytes 393220
  32.9 23.8 %copy-start.8 = (f32[4096]{0:T(1024)S(1)}, f32[4096]{0:T(1024)}, u32[]{:S(2)}) copy-start(f32[4096]{0:T(1024)} %param.18) | copy-start | bytes 49156
  32.9 26.0 %copy-start.9 = (f32[7,256]{1,0:T(8,128)S(1)}, f32[7,256]{1,0:T(8,128)}, u32[]{:S(2)}) copy-start(f32[7,256]{1,0:T(8,128)} %param.22) | copy-start | bytes 21508
  33.0 8.0 %collective-permute-start.14 = (bf16[64,1152]{1,0:T(8,128)(2,1)S(1)}, bf16[64,1152]{1,0:T(8,128)(2,1)S(1)}, u32[]{:S(2)}, u32[]{:S(2)}) collective-permute-start(bf16[64,1152]{1,0:T(8,128)(2,1)S(1)} %get-tuple-element.35), channel_id=1, source_target_pairs={{0,2},{1,3},{2,0},{3,1},{4,6},{5,7},{6,4},{7,5},{8,10},{9,11},{10,... | collective-permute-start | bytes 442376 | tf_op jit(solution)/shard_map/ppermute | solution.py:241
  34.6 8.9 %collective-permute-start.15 = (bf16[64,1152]{1,0:T(8,128)(2,1)S(1)}, bf16[64,1152]{1,0:T(8,128)(2,1)S(1)}, u32[]{:S(2)}, u32[]{:S(2)}) collective-permute-start(bf16[64,1152]{1,0:T(8,128)(2,1)S(1)} %get-tuple-element.34), channel_id=1, source_target_pairs={{0,4},{1,5},{2,6},{3,7},{4,0},{5,1},{6,2},{7,3},{8,12},{9,13},{10,... | collective-permute-start | bytes 442376 | tf_op jit(solution)/shard_map/ppermute | solution.py:241
  36.1 8.4 %collective-permute-start.16 = (bf16[64,1152]{1,0:T(8,128)(2,1)S(1)}, bf16[64,1152]{1,0:T(8,128)(2,1)S(1)}, u32[]{:S(2)}, u32[]{:S(2)}) collective-permute-start(bf16[64,1152]{1,0:T(8,128)(2,1)S(1)} %get-tuple-element.33), channel_id=1, source_target_pairs={{0,6},{1,7},{2,4},{3,5},{4,2},{5,3},{6,0},{7,1},{8,14},{9,15},{10,... | collective-permute-start | bytes 442376 | tf_op jit(solution)/shard_map/ppermute | solution.py:241
  36.5 10.1 %collective-permute-start.6 = (bf16[64,1152]{1,0:T(8,128)(2,1)S(1)}, bf16[64,1152]{1,0:T(8,128)(2,1)S(1)}, u32[]{:S(2)}, u32[]{:S(2)}) collective-permute-start(bf16[64,1152]{1,0:T(8,128)(2,1)S(1)} %get-tuple-element.39), channel_id=1, source_target_pairs={{0,2},{1,3},{2,0},{3,1},{4,6},{5,7},{6,4},{7,5},{8,10},{9,11},{10,... | collective-permute-start | bytes 442376 | tf_op jit(solution)/shard_map/ppermute | solution.py:241
  38.1 8.5 %collective-permute-start.7 = (bf16[64,1152]{1,0:T(8,128)(2,1)S(1)}, bf16[64,1152]{1,0:T(8,128)(2,1)S(1)}, u32[]{:S(2)}, u32[]{:S(2)}) collective-permute-start(bf16[64,1152]{1,0:T(8,128)(2,1)S(1)} %get-tuple-element.38), channel_id=1, source_target_pairs={{0,4},{1,5},{2,6},{3,7},{4,0},{5,1},{6,2},{7,3},{8,12},{9,13},{10,... | collective-permute-start | bytes 442376 | tf_op jit(solution)/shard_map/ppermute | solution.py:241
  41.0 7.1 %collective-permute-start.8 = (bf16[64,1152]{1,0:T(8,128)(2,1)S(1)}, bf16[64,1152]{1,0:T(8,128)(2,1)S(1)}, u32[]{:S(2)}, u32[]{:S(2)}) collective-permute-start(bf16[64,1152]{1,0:T(8,128)(2,1)S(1)} %get-tuple-element.37), channel_id=1, source_target_pairs={{0,6},{1,7},{2,4},{3,5},{4,2},{5,3},{6,0},{7,1},{8,14},{9,15},{10,... | collective-permute-start | bytes 442376 | tf_op jit(solution)/shard_map/ppermute | solution.py:241
  45.0 5.7 %collective-permute-start.17 = (bf16[64,1152]{1,0:T(8,128)(2,1)S(1)}, bf16[64,1152]{1,0:T(8,128)(2,1)S(1)}, u32[]{:S(2)}, u32[]{:S(2)}) collective-permute-start(bf16[64,1152]{1,0:T(8,128)(2,1)S(1)} %get-tuple-element.26), channel_id=1, source_target_pairs={{0,24},{4,28},{8,16},{12,20},{16,8},{20,12},{24,0},{28,4},{1,25},{... | collective-permute-start | bytes 442376 | tf_op jit(solution)/shard_map/ppermute | solution.py:20
  46.6 7.1 %collective-permute-start.18 = (bf16[64,1152]{1,0:T(8,128)(2,1)S(1)}, bf16[64,1152]{1,0:T(8,128)(2,1)S(1)}, u32[]{:S(2)}, u32[]{:S(2)}) collective-permute-start(bf16[64,1152]{1,0:T(8,128)(2,1)S(1)} %get-tuple-element.27), channel_id=1, source_target_pairs={{0,16},{4,20},{8,24},{12,28},{16,0},{20,4},{24,8},{28,12},{1,17},{... | collective-permute-start | bytes 442376 | tf_op jit(solution)/shard_map/ppermute | solution.py:20
  48.5 15.7 %copy-start.6 = (bf16[6,4096]{1,0:T(8,128)(2,1)S(1)}, bf16[6,4096]{1,0:T(8,128)(2,1)}, u32[]{:S(2)}) copy-start(bf16[6,4096]{1,0:T(8,128)(2,1)} %param.21) | copy-start | bytes 147460
  48.5 6.0 %collective-permute-start.19 = (bf16[64,1152]{1,0:T(8,128)(2,1)S(1)}, bf16[64,1152]{1,0:T(8,128)(2,1)S(1)}, u32[]{:S(2)}, u32[]{:S(2)}) collective-permute-start(bf16[64,1152]{1,0:T(8,128)(2,1)S(1)} %get-tuple-element.28), channel_id=1, source_target_pairs={{0,8},{4,12},{8,0},{12,4},{16,24},{20,28},{24,16},{28,20},{1,9},{5... | collective-permute-start | bytes 442376 | tf_op jit(solution)/shard_map/ppermute | solution.py:20
  55.1 9.2 %copy-start.4 = (bf16[16,4096]{1,0:T(8,128)(2,1)S(1)}, bf16[16,4096]{1,0:T(8,128)(2,1)}, u32[]{:S(2)}) copy-start(bf16[16,4096]{1,0:T(8,128)(2,1)} %param.20) | copy-start | bytes 393220
  55.1 9.2 %copy-start.7 = (f32[4096]{0:T(1024)S(1)}, f32[4096]{0:T(1024)}, u32[]{:S(2)}) copy-start(f32[4096]{0:T(1024)} %param.23) | copy-start | bytes 49156
  55.1 1.3 %collective-permute-start.20 = (bf16[2,16,1024]{2,1,0:T(8,128)(2,1)S(1)}, bf16[2,16,1024]{2,1,0:T(8,128)(2,1)S(1)}, u32[]{:S(2)}, u32[]{:S(2)}) collective-permute-start(bf16[2,16,1024]{2,1,0:T(8,128)(2,1)S(1)} %get-tuple-element.49), channel_id=1, source_target_pairs={{0,1},{1,0},{2,3},{3,2},{4,5},{5,4},{6,7},{7,6},{8,9},{9,8},{10,11... | collective-permute-start | bytes 196616 | tf_op jit(solution)/shard_map/ppermute | solution.py:20
  56.8 7.4 %collective-permute-start.21 = (bf16[6,4096]{1,0:T(8,128)(2,1)S(1)}, bf16[6,4096]{1,0:T(8,128)(2,1)S(1)}, u32[]{:S(2)}, u32[]{:S(2)}) collective-permute-start(bf16[6,4096]{1,0:T(8,128)(2,1)S(1)} %slice.231), channel_id=1, source_target_pairs={{0,1},{1,2},{2,3},{3,4},{4,5},{5,6},{6,7},{7,8},{8,9},{9,10},{10,1... | collective-permute-start | bytes 147464 | tf_op jit(solution)/shard_map/ppermute | solution.py:342
